TPU v7x, 32 devices: a whole 2x2x4 slice. The times are simulated.
32 devices in a mesh: rep: 8 (over y, x, core), fsdp: 4 (over z).
Axes of the slice: x: 2, y: 2, z: 4, core: 2. Of those that a mesh axis runs over, the one named last changes fastest.
Arguments:
- tokens: bfloat16 [16384, 1024], P(('rep', 'fsdp')), may hold values from -6 to 6
- cotangent: bfloat16 [16384, 1024], P(('rep', 'fsdp')), may hold values from -6 to 6
- valid_count: int32 [8, 4], P('rep', 'fsdp'), may hold values from 128 to 512, as said below
- norm_mix: bfloat16 [1024], P('fsdp'), may hold values from 0.5 to 1.5
- w_query: bfloat16 [1024, 1024], P('fsdp'), may hold values from -0.1875 to 0.1875
- w_key: bfloat16 [1024, 1024], P('fsdp'), may hold values from -0.1875 to 0.1875
- w_value: bfloat16 [1024, 2048], P('fsdp'), may hold values from -0.1875 to 0.1875
- w_gate: bfloat16 [1024, 2048], P('fsdp'), may hold values from -0.1875 to 0.1875
- w_beta: bfloat16 [1024, 8], P('fsdp'), may hold values from -0.1875 to 0.1875
- w_decay: bfloat16 [1024, 8], P('fsdp'), may hold values from -0.1875 to 0.1875
- a_log: float32 [8], replicated, may hold values from 0 to 2.77
- dt_bias: float32 [8], replicated, may hold values from -6.9 to -2.25
- conv_weight: bfloat16 [4, 4096], P(None, 'fsdp'), may hold values from -3 to 3
- norm_head: bfloat16 [256], P('fsdp'), may hold values from 0.5 to 1.5
- w_out: bfloat16 [2048, 1024], P('fsdp'), may hold values from -0.125 to 0.125
- norm_ffn: bfloat16 [1024], P('fsdp'), may hold values from 0.5 to 1.5
- w_ffgate: bfloat16 [1024, 2816], P(None, 'fsdp'), may hold values from -0.1875 to 0.1875
- w_ffup: bfloat16 [1024, 2816], P(None, 'fsdp'), may hold values from -0.1875 to 0.1875
- w_ffdown: bfloat16 [2816, 1024], P('fsdp'), may hold values from -0.109375 to 0.109375
Outputs:
- output: bfloat16 [16384, 1024], P(('rep', 'fsdp'))
- grad_tokens: float32 [16384, 1024], P(('rep', 'fsdp'))
- grad_norm_mix: float32 [1024], P('fsdp')
- grad_query: float32 [1024, 1024], P('fsdp')
- grad_key: float32 [1024, 1024], P('fsdp')
- grad_value: float32 [1024, 2048], P('fsdp')
- grad_gate: float32 [1024, 2048], P('fsdp')
- grad_beta: float32 [1024, 8], P('fsdp')
- grad_decay: float32 [1024, 8], P('fsdp')
- grad_a_log: float32 [8], replicated
- grad_dt_bias: float32 [8], replicated
- grad_conv: float32 [4, 4096], P(None, 'fsdp')
- grad_norm_head: float32 [256], P('fsdp')
- grad_out: float32 [2048, 1024], P('fsdp')
- grad_norm_ffn: float32 [1024], P('fsdp')
- grad_ffgate: float32 [1024, 2816], P(None, 'fsdp')
- grad_ffup: float32 [1024, 2816], P(None, 'fsdp')
- grad_ffdown: float32 [2816, 1024], P('fsdp')
Inputs may be any that keep to these rules, and one draw needn't show every extreme that they name: Each device's rows below valid_count hold its part of its rep index's sequence; in every rep index one device has 512 valid rows and another has 128.
All inputs are finite; a program needn't handle non-finite values.
Results may differ from a plain program's by a relative error of at most 0.017.
Values may be sent and summed in bfloat16 or wider, within the bound.
No kernel may reach another device: no remote copies, remote signals or barrier semaphores. Data moves between devices by JAX's collectives and lax.ppermute only.
A program may use at most 384 MiB of HBM per device.

v0:
```python
import jax
import jax.numpy as jnp
from jax import lax
from jax.sharding import PartitionSpec as P

DK = 128
DV = 256
KW = 4
BLOCK = 64


norm_epsilon = 1e-06
head_epsilon = 1e-05
highest = lax.Precision.HIGHEST


def passed_along(block, axis, distance):
    devices = range(lax.axis_size(axis))
    route = [(i - distance, i) for i in devices if i - distance in devices]
    return lax.ppermute(block, axis, route)


def carried_in(value, axis, join, neutral, backward):
    count, mine = (lax.axis_size(axis), lax.axis_index(axis))
    pieces = jax.tree.map(lambda part: lax.all_gather(part, axis), value)
    if backward:
        pieces = jax.tree.map(lambda part: part[::-1], pieces)
        mine = count - 1 - mine
    running = jax.tree.map(
        lambda part, zero: jnp.full_like(part, 0) + jnp.asarray(zero, part.dtype), value, neutral
    )

    def hop(position, running):
        longer = join(running, jax.tree.map(lambda part: part[position], pieces))
        return jax.tree.map(lambda new, old: jnp.where(position < mine, new, old), longer, running)

    return lax.fori_loop(0, count - 1, hop, running)


def matmul_low(left, right):
    return jnp.dot(left, right, preferred_element_type=jnp.float32)


def matmul_high(left, right):
    return jnp.dot(left, right, precision=highest, preferred_element_type=jnp.float32)


def rms_scale(values, gain):
    return values * lax.rsqrt(jnp.mean(values * values, -1, keepdims=True) + norm_epsilon) * gain


def swiglu(ff_gate, ff_up):
    return jax.nn.silu(ff_gate) * ff_up


def mixer_front(projected, previous, conv_full, beta_pre, decay_pre, a_log, dt_bias, valid_mask):
    row_count = projected.shape[0]
    head_count = a_log.shape[0]
    extended = jnp.concatenate([previous, projected], 0)
    convolved = conv_full[0] * extended[0:row_count]
    for j in range(1, KW):
        convolved = convolved + conv_full[j] * extended[j : j + row_count]
    activated = jax.nn.silu(convolved)
    qk_width = head_count * DK
    queries = activated[:, :qk_width].reshape(row_count, head_count, DK)
    key_vecs = activated[:, qk_width : 2 * qk_width].reshape(row_count, head_count, DK)
    values = activated[:, 2 * qk_width :].reshape(row_count, head_count, DV)
    queries = (
        queries
        * lax.rsqrt(jnp.sum(queries * queries, -1, keepdims=True) + norm_epsilon)
        * DK ** (-0.5)
    )
    key_vecs = key_vecs * lax.rsqrt(jnp.sum(key_vecs * key_vecs, -1, keepdims=True) + norm_epsilon)
    beta_gate = valid_mask * jax.nn.sigmoid(beta_pre)
    log_decay = -valid_mask * jnp.exp(a_log) * jax.nn.softplus(decay_pre + dt_bias)
    return (queries, key_vecs, values, beta_gate, log_decay)


def to_blocks(values):
    row_count, head_count, inner = values.shape
    return values.reshape(row_count // BLOCK, BLOCK, head_count, inner).transpose(0, 2, 1, 3)


def to_heads(values):
    row_count, head_count = values.shape
    return values.reshape(row_count // BLOCK, BLOCK, head_count).transpose(0, 2, 1)


def block_parts(key_vecs, values, beta_gate, log_decay):
    keys_b = to_blocks(key_vecs)
    values_b = to_blocks(values)
    betas_b = to_heads(beta_gate)
    cum_log = jnp.cumsum(to_heads(log_decay), -1)
    places = jnp.arange(BLOCK)
    below_mask = places[:, None] > places[None, :]
    gap_log = cum_log[..., :, None] - cum_log[..., None, :]
    decay_mask = jnp.where(below_mask, jnp.exp(jnp.where(below_mask, gap_log, 0.0)), 0.0)
    key_inner = jnp.einsum("nhid,nhjd->nhij", keys_b, keys_b, precision=highest)
    system = jnp.eye(BLOCK, dtype=jnp.float32) + betas_b[..., :, None] * key_inner * decay_mask
    wy_keys = jax.scipy.linalg.solve_triangular(
        system, (betas_b * jnp.exp(cum_log))[..., None] * keys_b, lower=True, unit_diagonal=True
    )
    wy_values = jax.scipy.linalg.solve_triangular(
        system, betas_b[..., None] * values_b, lower=True, unit_diagonal=True
    )
    key_tilde = jnp.exp(cum_log[..., -1:] - cum_log)[..., None] * keys_b
    return (cum_log, wy_keys, wy_values, key_tilde)


def block_outputs(queries, key_vecs, cum_log, wy_keys, wy_values, key_tilde, start_state):
    row_count, head_count = (queries.shape[0], queries.shape[1])
    places = jnp.arange(BLOCK)
    within = places[:, None] >= places[None, :]

    def block_step(carried, pieces):
        query_b, key_b, cum_b, wkey_b, wval_b, ktil_b = pieces
        fresh_values = wval_b - jnp.einsum("hcd,hde->hce", wkey_b, carried, precision=highest)
        gap_log = cum_b[:, :, None] - cum_b[:, None, :]
        decay_mask = jnp.where(within, jnp.exp(jnp.where(within, gap_log, 0.0)), 0.0)
        scores = jnp.einsum("hid,hjd->hij", query_b, key_b, precision=highest) * decay_mask
        result = jnp.exp(cum_b)[..., None] * jnp.einsum(
            "hcd,hde->hce", query_b, carried, precision=highest
        )
        result = result + jnp.einsum("hij,hje->hie", scores, fresh_values, precision=highest)
        next_state = jnp.exp(cum_b[:, -1])[:, None, None] * carried + jnp.einsum(
            "hcd,hce->hde", ktil_b, fresh_values, precision=highest
        )
        return (next_state, result)

    final_state, results = lax.scan(
        jax.checkpoint(block_step),
        start_state,
        (to_blocks(queries), to_blocks(key_vecs), cum_log, wy_keys, wy_values, key_tilde),
    )
    mixed_heads = results.transpose(0, 2, 1, 3).reshape(row_count, head_count * DV)
    return (mixed_heads, final_state)


def device_map(cum_log, wy_keys, wy_values, key_tilde):
    head_count = cum_log.shape[1]
    identity = jnp.broadcast_to(jnp.eye(DK, dtype=jnp.float32), (head_count, DK, DK))

    def compose(carried, pieces):
        transit, offset = carried
        cum_b, wkey_b, wval_b, ktil_b = pieces
        block_transit = jnp.exp(cum_b[:, -1])[:, None, None] * identity - jnp.einsum(
            "hcd,hce->hde", ktil_b, wkey_b, precision=highest
        )
        block_offset = jnp.einsum("hcd,hce->hde", ktil_b, wval_b, precision=highest)
        new_transit = jnp.einsum("hde,hef->hdf", block_transit, transit, precision=highest)
        new_offset = (
            jnp.einsum("hde,hef->hdf", block_transit, offset, precision=highest) + block_offset
        )
        return ((new_transit, new_offset), None)

    initial = (identity, jnp.zeros((head_count, DK, DV), jnp.float32))
    (transit, offset), _ = lax.scan(compose, initial, (cum_log, wy_keys, wy_values, key_tilde))
    return (transit, offset)


def combine_maps(earlier, later):
    return (
        jnp.einsum("hde,hef->hdf", later[0], earlier[0], precision=highest),
        jnp.einsum("hde,hef->hdf", later[0], earlier[1], precision=highest) + later[1],
    )


def local_delta(queries, key_vecs, values, beta_gate, log_decay, start_state):
    cum_log, wy_keys, wy_values, key_tilde = block_parts(key_vecs, values, beta_gate, log_decay)
    return block_outputs(queries, key_vecs, cum_log, wy_keys, wy_values, key_tilde, start_state)


def gate_tail(mixed_heads, gate_pre, head_gain):
    row_count = mixed_heads.shape[0]
    per_head = mixed_heads.reshape(row_count, -1, DV)
    scaled = (
        per_head
        * lax.rsqrt(jnp.mean(per_head * per_head, -1, keepdims=True) + head_epsilon)
        * head_gain
    )
    return scaled.reshape(row_count, -1) * jax.nn.silu(gate_pre)


def gather_mixer(
    norm_mix,
    w_query,
    w_key,
    w_value,
    w_gate,
    w_beta,
    w_decay,
    conv_weight,
    norm_head,
    w_out,
    norm_ffn,
):
    return (
        lax.all_gather(norm_mix, "fsdp", axis=0, tiled=True),
        lax.all_gather(w_query, "fsdp", axis=0, tiled=True),
        lax.all_gather(w_key, "fsdp", axis=0, tiled=True),
        lax.all_gather(w_value, "fsdp", axis=0, tiled=True),
        lax.all_gather(w_gate, "fsdp", axis=0, tiled=True),
        lax.all_gather(w_beta, "fsdp", axis=0, tiled=True),
        lax.all_gather(w_decay, "fsdp", axis=0, tiled=True),
        lax.all_gather(conv_weight, "fsdp", axis=1, tiled=True),
        lax.all_gather(norm_head, "fsdp", axis=0, tiled=True),
        lax.all_gather(w_out, "fsdp", axis=0, tiled=True),
        lax.all_gather(norm_ffn, "fsdp", axis=0, tiled=True),
    )


def on_device(
    tokens,
    cotangent,
    valid_count,
    norm_mix,
    w_query,
    w_key,
    w_value,
    w_gate,
    w_beta,
    w_decay,
    a_log,
    dt_bias,
    conv_weight,
    norm_head,
    w_out,
    norm_ffn,
    w_ffgate,
    w_ffup,
    w_ffdown,
):
    row_count = tokens.shape[0]
    own_count = valid_count[0, 0]
    valid_mask = (jnp.arange(row_count) < own_count).astype(jnp.float32)[:, None]
    inputs = tokens.astype(jnp.float32)
    mixer_full = gather_mixer(
        norm_mix,
        w_query,
        w_key,
        w_value,
        w_gate,
        w_beta,
        w_decay,
        conv_weight,
        norm_head,
        w_out,
        norm_ffn,
    )
    normed_f32, mix_pull = jax.vjp(rms_scale, inputs, mixer_full[0].astype(jnp.float32))
    normed = normed_f32.astype(jnp.bfloat16)
    projected = jnp.concatenate(
        [
            matmul_low(normed, mixer_full[1]),
            matmul_low(normed, mixer_full[2]),
            matmul_low(normed, mixer_full[3]),
        ],
        1,
    )
    gate_pre = matmul_low(normed, mixer_full[4])
    beta_pre = matmul_low(normed, mixer_full[5])
    decay_pre = matmul_low(normed, mixer_full[6])
    edge_place = own_count - (KW - 1)
    tail_rows = lax.dynamic_slice_in_dim(projected, edge_place, KW - 1, 0)
    previous = passed_along(tail_rows, "fsdp", 1)

    def front_local(projected_in, previous_in, conv_in, beta_in, decay_in, log_rate, bias_in):
        return mixer_front(
            projected_in, previous_in, conv_in, beta_in, decay_in, log_rate, bias_in, valid_mask
        )

    front_values, front_pull = jax.vjp(
        front_local,
        projected,
        previous,
        mixer_full[7].astype(jnp.float32),
        beta_pre,
        decay_pre,
        a_log,
        dt_bias,
    )
    queries, key_vecs, values, beta_gate, log_decay = front_values
    cum_log, wy_keys, wy_values, key_tilde = block_parts(key_vecs, values, beta_gate, log_decay)
    transit, offset = device_map(cum_log, wy_keys, wy_values, key_tilde)
    eye_state = jnp.broadcast_to(jnp.eye(DK, dtype=jnp.float32), transit.shape)
    zero_state = jnp.zeros_like(offset)
    prefix = carried_in((transit, offset), "fsdp", combine_maps, (eye_state, zero_state), False)
    start_state = prefix[1]
    delta_out, delta_pull = jax.vjp(
        local_delta, queries, key_vecs, values, beta_gate, log_decay, start_state
    )
    mixed_heads = delta_out[0]
    gated_f32, tail_pull = jax.vjp(
        gate_tail, mixed_heads, gate_pre, mixer_full[8].astype(jnp.float32)
    )
    gated_out = gated_f32.astype(jnp.bfloat16)
    residual = inputs + matmul_low(gated_out, mixer_full[9])
    ffn_f32, ffn_pull = jax.vjp(rms_scale, residual, mixer_full[10].astype(jnp.float32))
    normed_ffn = ffn_f32.astype(jnp.bfloat16)
    ffn_rows = lax.all_gather(normed_ffn, "fsdp", axis=0, tiled=True)
    swiglu_f32, swiglu_pull = jax.vjp(
        swiglu, matmul_low(ffn_rows, w_ffgate), matmul_low(ffn_rows, w_ffup)
    )
    swiglu_out = swiglu_f32.astype(jnp.bfloat16)
    ffn_out = lax.psum_scatter(
        matmul_low(swiglu_out, w_ffdown).astype(jnp.bfloat16),
        "fsdp",
        scatter_dimension=0,
        tiled=True,
    ).astype(jnp.float32)
    output = (valid_mask * (residual + ffn_out)).astype(jnp.bfloat16)
    out_grad = cotangent.astype(jnp.float32) * valid_mask
    out_low = out_grad.astype(jnp.bfloat16)
    grad_rows = lax.all_gather(out_low, "fsdp", axis=0, tiled=True)
    gate_grad_f32, up_grad_f32 = swiglu_pull(matmul_low(grad_rows, w_ffdown.T))
    gate_low = gate_grad_f32.astype(jnp.bfloat16)
    up_low = up_grad_f32.astype(jnp.bfloat16)
    ffgate_grad = matmul_low(ffn_rows.T, gate_low)
    ffup_grad = matmul_low(ffn_rows.T, up_low)
    ffdown_grad = matmul_low(swiglu_out.T, grad_rows)
    ffn_in_grad = lax.psum_scatter(
        matmul_low(gate_low, w_ffgate.T) + matmul_low(up_low, w_ffup.T),
        "fsdp",
        scatter_dimension=0,
        tiled=True,
    )
    residual_part, ffn_gain_grad = ffn_pull(ffn_in_grad)
    residual_grad = out_grad + residual_part
    residual_low = residual_grad.astype(jnp.bfloat16)
    out_weight_grad = matmul_low(gated_out.T, residual_low)
    mixed_grad, gate_pre_grad, head_gain_grad = tail_pull(matmul_low(residual_low, mixer_full[9].T))
    gate_mix_low = gate_pre_grad.astype(jnp.bfloat16)

    def state_only(carried):
        return block_outputs(queries, key_vecs, cum_log, wy_keys, wy_values, key_tilde, carried)[0]

    _, state_pull = jax.vjp(state_only, start_state)
    own_state_grad = state_pull(mixed_grad)[0]
    suffix = carried_in(
        (jnp.swapaxes(transit, 1, 2), own_state_grad),
        "fsdp",
        combine_maps,
        (eye_state, zero_state),
        True,
    )
    delta_grads = delta_pull((mixed_grad, suffix[1]))
    front_grads = front_pull(
        (delta_grads[0], delta_grads[1], delta_grads[2], delta_grads[3], delta_grads[4])
    )
    (
        projected_grad,
        previous_grad,
        conv_grad,
        beta_pre_grad,
        decay_pre_grad,
        log_rate_grad,
        bias_grad,
    ) = front_grads
    coming = passed_along(previous_grad.astype(jnp.bfloat16), "fsdp", -1).astype(
        previous_grad.dtype
    )
    edge_rows = lax.dynamic_slice_in_dim(projected_grad, edge_place, KW - 1, 0) + coming
    projected_grad = lax.dynamic_update_slice_in_dim(projected_grad, edge_rows, edge_place, 0)
    projected_low = projected_grad.astype(jnp.bfloat16)
    qk_width = a_log.shape[0] * DK
    query_low = projected_low[:, :qk_width]
    key_low = projected_low[:, qk_width : 2 * qk_width]
    value_low = projected_low[:, 2 * qk_width :]
    normed_grad = (
        matmul_low(query_low, mixer_full[1].T)
        + matmul_low(key_low, mixer_full[2].T)
        + matmul_low(value_low, mixer_full[3].T)
    )
    normed_grad = normed_grad + matmul_low(gate_mix_low, mixer_full[4].T)
    normed_grad = (
        normed_grad
        + matmul_high(beta_pre_grad, mixer_full[5].astype(jnp.float32).T)
        + matmul_high(decay_pre_grad, mixer_full[6].astype(jnp.float32).T)
    )
    input_part, mix_gain_grad = mix_pull(normed_grad)
    grad_tokens = residual_grad + input_part
    normed_wide = normed.astype(jnp.float32)
    shards = (
        lax.psum_scatter(
            mix_gain_grad.astype(jnp.bfloat16), "fsdp", scatter_dimension=0, tiled=True
        ).astype(jnp.float32),
        lax.psum_scatter(
            matmul_low(normed.T, query_low).astype(jnp.bfloat16),
            "fsdp",
            scatter_dimension=0,
            tiled=True,
        ).astype(jnp.float32),
        lax.psum_scatter(
            matmul_low(normed.T, key_low).astype(jnp.bfloat16),
            "fsdp",
            scatter_dimension=0,
            tiled=True,
        ).astype(jnp.float32),
        lax.psum_scatter(
            matmul_low(normed.T, value_low).astype(jnp.bfloat16),
            "fsdp",
            scatter_dimension=0,
            tiled=True,
        ).astype(jnp.float32),
        lax.psum_scatter(
            matmul_low(normed.T, gate_mix_low).astype(jnp.bfloat16),
            "fsdp",
            scatter_dimension=0,
            tiled=True,
        ).astype(jnp.float32),
        lax.psum_scatter(
            matmul_high(normed_wide.T, beta_pre_grad).astype(jnp.bfloat16),
            "fsdp",
            scatter_dimension=0,
            tiled=True,
        ).astype(jnp.float32),
        lax.psum_scatter(
            matmul_high(normed_wide.T, decay_pre_grad).astype(jnp.bfloat16),
            "fsdp",
            scatter_dimension=0,
            tiled=True,
        ).astype(jnp.float32),
        lax.psum_scatter(
            conv_grad.astype(jnp.bfloat16), "fsdp", scatter_dimension=1, tiled=True
        ).astype(jnp.float32),
        lax.psum_scatter(
            head_gain_grad.astype(jnp.bfloat16), "fsdp", scatter_dimension=0, tiled=True
        ).astype(jnp.float32),
        lax.psum_scatter(
            out_weight_grad.astype(jnp.bfloat16), "fsdp", scatter_dimension=0, tiled=True
        ).astype(jnp.float32),
        lax.psum_scatter(
            ffn_gain_grad.astype(jnp.bfloat16), "fsdp", scatter_dimension=0, tiled=True
        ).astype(jnp.float32),
    )
    summed = (
        lax.psum(shards[0].astype(jnp.bfloat16), "rep").astype(jnp.float32),
        lax.psum(shards[1].astype(jnp.bfloat16), "rep").astype(jnp.float32),
        lax.psum(shards[2].astype(jnp.bfloat16), "rep").astype(jnp.float32),
        lax.psum(shards[3].astype(jnp.bfloat16), "rep").astype(jnp.float32),
        lax.psum(shards[4].astype(jnp.bfloat16), "rep").astype(jnp.float32),
        lax.psum(shards[5].astype(jnp.bfloat16), "rep").astype(jnp.float32),
        lax.psum(shards[6].astype(jnp.bfloat16), "rep").astype(jnp.float32),
        lax.psum(shards[7].astype(jnp.bfloat16), "rep").astype(jnp.float32),
        lax.psum(shards[8].astype(jnp.bfloat16), "rep").astype(jnp.float32),
        lax.psum(shards[9].astype(jnp.bfloat16), "rep").astype(jnp.float32),
        lax.psum(shards[10].astype(jnp.bfloat16), "rep").astype(jnp.float32),
        lax.psum(ffgate_grad.astype(jnp.bfloat16), "rep").astype(jnp.float32),
        lax.psum(ffup_grad.astype(jnp.bfloat16), "rep").astype(jnp.float32),
        lax.psum(ffdown_grad.astype(jnp.bfloat16), "rep").astype(jnp.float32),
    )
    rate_sums = lax.psum((log_rate_grad, bias_grad), ("rep", "fsdp"))
    return (
        output,
        grad_tokens,
        summed[0],
        summed[1],
        summed[2],
        summed[3],
        summed[4],
        summed[5],
        summed[6],
        rate_sums[0],
        rate_sums[1],
        summed[7],
        summed[8],
        summed[9],
        summed[10],
        summed[11],
        summed[12],
        summed[13],
    )


def solution(mesh):
    placed = (
        P(("rep", "fsdp"), None),
        P(("rep", "fsdp"), None),
        P("rep", "fsdp"),
        P("fsdp"),
        P("fsdp", None),
        P("fsdp", None),
        P("fsdp", None),
        P("fsdp", None),
        P("fsdp", None),
        P("fsdp", None),
        P(),
        P(),
        P(None, "fsdp"),
        P("fsdp"),
        P("fsdp", None),
        P("fsdp"),
        P(None, "fsdp"),
        P(None, "fsdp"),
        P("fsdp", None),
    )
    return jax.shard_map(
        on_device,
        mesh=mesh,
        in_specs=placed,
        out_specs=(
            P(("rep", "fsdp"), None),
            P(("rep", "fsdp"), None),
            P("fsdp"),
            P("fsdp", None),
            P("fsdp", None),
            P("fsdp", None),
            P("fsdp", None),
            P("fsdp", None),
            P("fsdp", None),
            P(),
            P(),
            P(None, "fsdp"),
            P("fsdp"),
            P("fsdp", None),
            P("fsdp"),
            P(None, "fsdp"),
            P(None, "fsdp"),
            P("fsdp", None),
        ),
        check_vma=False,
    )
```

profile of v0, /device:TPU:0, one launch (start us, length us, event | category | flops | bytes accessed | tf_op | source)
XLA Modules:
  0.0 2275.0 jit_solution(16961187328285449372)
XLA Ops:
  10.2 12.6 all-gather.4
  22.9 13.4 all_gather.64
  37.8 13.2 all_gather.69
  53.9 13.1 all_gather.65
  73.2 32.2 %all-gather.18.cloned.1.call-done = bf16[1024,1024]{1,0:T(8,128)(2,1)} async-done(((bf16[256,1024]{1,0:T(8,128)(2,1)}), bf16[1024,1024]{1,0:T(8,128)(2,1)}) %all-gather.18.cloned.1.call-update) | async-done | bytes 2097168 | tf_op jit(solution)/shard_map/all_gather | solution.py:199
  109.9 76.5 %all-gather.22.cloned.1.call-done = bf16[1024,2048]{1,0:T(8,128)(2,1)} async-done(((bf16[256,2048]{1,0:T(8,128)(2,1)}), bf16[1024,2048]{1,0:T(8,128)(2,1)}) %all-gather.22.cloned.1.call-update) | async-done | bytes 4194320 | tf_op jit(solution)/shard_map/all_gather | solution.py:201
  206.0 18.7 fusion.101
  250.8 315.7 %custom-call.22 = f32[8,8,1,64,64]{3,4,2,1,0:T(8,128)S(1)} custom-call(f32[8,8,1,64,64]{4,3,2,1,0:T(8,128)} %add_bitcast_fusion), custom_call_target="InvertDiagBlocksLowerTriangular" | custom-call | tf_op jit(solution)/shard_map/jit(_solve_triangular)/vmap(vmap())/triangular_solve/custom-call.1 | solution.py:100
  571.4 8.5 fusion.133
  579.9 6.7 fusion.110
  586.6 63.0 %while.103 = (s32[]{:T(128)}, f32[8,128,128]{2,1,0:T(8,128)S(1)}, f32[8,128,256]{2,1,0:T(8,128)}, f32[8,8,64]{1,2,0:T(8,128)}, f32[8,8,64,128]{3,2,1,0:T(8,128)}...) while((s32[]{:T(128)}, f32[8,128,128]{2,1,0:T(8,128)S(1)}, ...), condition=%wide.region_4.7_spmd.clone, body=%wide.region_3.0_spmd.clone.sunk | while | flops 906756096 | bytes 13441271 | solution.py:157
  654.0 10.0 all-reduce.13
  664.6 9.0 all-gather.5
  681.6 14.3 all-gather.32.cloned.1.call-done
  695.9 81.4 %all-gather.34.cloned.1.call-done = f32[32,128,256]{2,1,0:T(8,128)} async-done(((f32[8,128,256]{2,1,0:T(8,128)}), f32[32,128,256]{2,1,0:T(8,128)}) %all-gather.34.cloned.1.call-update) | async-done | bytes 4194320 | tf_op jit(solution)/shard_map/all_gather | solution.py:25
  777.3 8.0 while.104
  787.9 103.2 %while.102 = (s32[]{:T(128)}, f32[8,128,256]{2,1,0:T(8,128)S(1)}, f32[8,8,64,256]{3,2,1,0:T(8,128)}, f32[8,8,128,256]{3,2,1,0:T(8,128)}, f32[8,8,64]{1,2,0:T(8,1...) while((s32[]{:T(128)}, f32[8,128,256]{2,1,0:T(8,128)S(1)}, ...), condition=%wide.region_9.12_spmd.clone.clone, body=%wide.region_8.11_spmd.clone.clone.sunk | while | flops 756023296 | bytes 11578629 | solution.py:130
  905.7 9.3 multiply_convert_fusion.2
  915.0 23.9 %all-gather.26.cloned.1.call-done = bf16[2048,1024]{1,0:T(8,128)(2,1)} async-done(((bf16[512,1024]{1,0:T(8,128)(2,1)}), bf16[2048,1024]{1,0:T(8,128)(2,1)}) %all-gather.26.cloned.1.call-update) | async-done | bytes 4194320 | tf_op jit(solution)/shard_map/all_gather | solution.py:207
  949.3 76.4 %all-gather.28.cloned.1.call-done = bf16[2048,1024]{1,0:T(8,128)(2,1)} async-done(((bf16[512,1024]{1,0:T(8,128)(2,1)}), bf16[2048,1024]{1,0:T(8,128)(2,1)}) %all-gather.28.cloned.1.call-update) | async-done | bytes 4194320 | tf_op jit(solution)/shard_map/all_gather | solution.py:300
  1025.7 8.5 fusion.223
  1039.3 67.9 %all-gather.30.cloned.1.call-done = bf16[2048,1024]{1,0:T(8,128)(2,1)} async-done(((bf16[512,1024]{1,0:T(8,128)(2,1)}), bf16[2048,1024]{1,0:T(8,128)(2,1)}) %all-gather.30.cloned.1.call-update) | async-done | bytes 4194320 | tf_op jit(solution)/shard_map/all_gather | solution.py:314
  1107.2 10.5 multiply_convert_fusion
  1127.3 7.0 convolution_convert_fusion.3
  1136.4 133.8 %reduce-scatter.15.cloned.1.call-done = f32[512,1024]{1,0:T(8,128)} async-done(((f32[2048,1024]{1,0:T(8,128)}), f32[512,1024]{1,0:T(8,128)}) %reduce-scatter.15.cloned.1.call-update) | async-done | bytes 2097168 | tf_op jit(solution)/shard_map/reduce_scatter | solution.py:321
  1272.9 77.1 %reduce-scatter.13.cloned.1.call-done = bf16[512,1024]{1,0:T(8,128)(2,1)} async-done(((bf16[2048,1024]{1,0:T(8,128)(2,1)}), bf16[512,1024]{1,0:T(8,128)(2,1)}) %reduce-scatter.13.cloned.1.call-update) | async-done | bytes 1048592 | tf_op jit(solution)/shard_map/reduce_scatter | solution.py:305
  1354.9 7.4 multiply_reduce_fusion.5
  1368.9 89.8 %while.105 = (s32[]{:T(128)}, f32[8,128,256]{2,1,0:T(8,128)}, f32[8,8,64,128]{3,2,1,0:T(8,128)}, f32[8,8,64,128]{3,2,1,0:T(8,128)}, f32[8,8,64]{1,2,0:T(8,128)},...) while((s32[]{:T(128)}, f32[8,128,256]{2,1,0:T(8,128)}, ...), condition=%wide.region_17.20_spmd.clone, body=%wide.region_16.19_spmd.clone.sunk | while | flops 756551680 | bytes 16281879 | solution.py:130
  1459.0 6.5 convolution_convert_fusion.1
  1476.5 63.7 %all-gather.38.cloned.1.call-done = f32[32,128,256]{2,1,0:T(8,128)} async-done(((f32[8,128,256]{2,1,0:T(8,128)}), f32[32,128,256]{2,1,0:T(8,128)}) %all-gather.38.cloned.1.call-update) | async-done | bytes 4194320 | tf_op jit(solution)/shard_map/all_gather | solution.py:25
  1544.9 8.0 while.106
  1561.7 177.7 %while.101 = (s32[]{:T(128)}, f32[8,128,256]{2,1,0:T(8,128)S(1)}, f32[8,8,64,128]{3,1,2,0:T(8,128)}, f32[8,8,64,128]{3,2,1,0:T(8,128)}, f32[8,8,64]{2,1,0:T(8,12...) while((s32[]{:T(128)}, f32[8,128,256]{2,1,0:T(8,128)S(1)}, ...), condition=%wide.region_25.28_spmd.clone, body=%wide.region_20.27_spmd.clone.sunk | while | flops 1966019584 | bytes 36389460 | solution.py:130
  1769.2 7.9 add_bitcast_fusion.1
  1783.7 8.9 fusion.111
  1807.7 11.8 add_add_fusion.3
  1819.6 12.8 multiply_reduce_fusion.3
  1832.4 14.5 broadcast_multiply_fusion
  1846.9 12.7 pad_add_fusion
  1886.8 7.4 convolution_convert_fusion.7
  1907.4 7.3 convolution_convert_fusion.8
  1914.7 6.5 reduce-scatter.17.cloned.1.call-done
  1921.2 45.9 %reduce-scatter.19.cloned.1.call-done = bf16[256,1024]{1,0:T(8,128)(2,1)} async-done(((bf16[1024,1024]{1,0:T(8,128)(2,1)}), bf16[256,1024]{1,0:T(8,128)(2,1)}) %reduce-scatter.19.cloned.1.call-update) | async-done | bytes 524304 | tf_op jit(solution)/shard_map/reduce_scatter | solution.py:393
  1967.1 78.4 %reduce-scatter.21.cloned.1.call-done = bf16[256,2048]{1,0:T(8,128)(2,1)} async-done(((bf16[1024,2048]{1,0:T(8,128)(2,1)}), bf16[256,2048]{1,0:T(8,128)(2,1)}) %reduce-scatter.21.cloned.1.call-update) | async-done | bytes 1048592 | tf_op jit(solution)/shard_map/reduce_scatter | solution.py:399
  2046.9 6.5 fusion.228
  2053.4 41.5 %all-reduce.17 = (f32[8]{0:T(128)}, f32[8]{0:T(128)}) all-reduce(f32[8]{0:T(128)S(1)} %exponential_multiply_fusion.1, f32[8]{0:T(128)S(1)} %get-tuple-element.1530), channel_id=1, replica_groups=mesh['rep'=8,'fsdp'=4] {'rep','fsdp'}, use_global_device_ids=true, to_apply=%region_53.57 | all-reduce | flops 16 | bytes 128 | tf_op jit(solution)/shard_map/psum | solution.py:452
  2106.1 10.3 all-reduce.20
  2121.3 24.1 %all-reduce.18 = (bf16[256]{0:T(256)(128)(2,1)S(1)}, bf16[256,8]{0,1:T(8,128)(2,1)S(1)}, bf16[256,8]{0,1:T(8,128)(2,1)S(1)}, bf16[4,1024]{1,0:T(4,128)(2,1)S(1)}...) all-reduce(bf16[256]{0:T(256)(128)(2,1)S(1)} %dynamic-slice.2, ...), channel_id=1, replica_groups=mesh['rep'=8,'fsdp'=4] {'rep'}, use_global_device_ids=true, to_apply=%region_39.43 | all-reduce | flops 8768 | bytes 35072 | tf_op jit(solution)/shard_map/psum | solution.py:437
  2148.9 103.9 %all-reduce.23.cloned.1.call-done = (bf16[256,1024]{1,0:T(8,128)(2,1)}, bf16[256,1024]{1,0:T(8,128)(2,1)}, bf16[256,2048]{1,0:T(8,128)(2,1)}, bf16[256,2048]{1,0...) async-done(((bf16[256,1024]{1,0:T(8,128)(2,1)}, bf16[256,1024]{1,0:T(8,128)(2,1)}, ...) | async-done | bytes 8519696 | tf_op jit(solution)/shard_map/psum | solution.py:438
  (1074 shorter events, 734.5 us)
Async XLA Ops:
  7.2 1100.0 %copy-start = (bf16[704,1024]{1,0:T(8,128)(2,1)S(1)}, bf16[704,1024]{1,0:T(8,128)(2,1)}, u32[]{:S(2)}) copy-start(bf16[704,1024]{1,0:T(8,128)(2,1)} %param.55) | copy-start | bytes 4325380
  7.2 15.6 copy-start.116
  7.2 29.0 %copy-start.31 = (bf16[512,1024]{1,0:T(8,128)(2,1)S(1)}, bf16[512,1024]{1,0:T(8,128)(2,1)}, u32[]{:S(2)}) copy-start(bf16[512,1024]{1,0:T(8,128)(2,1)} %param.37) | copy-start | bytes 3145732
  7.3 29.3 %copy-start.129 = (f32[8]{0:T(128)S(1)}, f32[8]{0:T(128)}, u32[]{:S(2)}) copy-start(f32[8]{0:T(128)} %param.48) | copy-start | bytes 100
  7.3 62.7 %all-gather.20.cloned.1.call-start = ((), (), s32[]{:S(2)}) async-start(), calls=%async_computation.11 | async-start | bytes 2621440 | tf_op jit(solution)/shard_map/all_gather | solution.py:200
  8.0 97.4 %all-gather.18.cloned.1.call-start = ((), (), s32[]{:S(2)}) async-start(), calls=%async_computation.10 | async-start | bytes 2621440 | tf_op jit(solution)/shard_map/all_gather | solution.py:199
  8.7 29.0 %copy-start.117 = (bf16[256,8]{0,1:T(8,128)(2,1)S(1)}, bf16[256,8]{0,1:T(8,128)(2,1)}, u32[]{:S(2)}) copy-start(bf16[256,8]{0,1:T(8,128)(2,1)} %param.45) | copy-start | bytes 12292
  8.8 177.7 %all-gather.22.cloned.1.call-start = ((), (), s32[]{:S(2)}) async-start(), calls=%async_computation.12 | async-start | bytes 5242880 | tf_op jit(solution)/shard_map/all_gather | solution.py:201
  9.5 686.4 %all-gather.32.cloned.1.call-start = ((), (), s32[]{:S(2)}) async-start(), calls=%async_computation.26 | async-start | bytes 2621440 | tf_op jit(solution)/shard_map/all_gather | solution.py:25
  9.6 28.1 %copy-start.119 = (f32[8]{0:T(128)}, f32[8]{0:T(128)S(1)}, u32[]{:S(2)}) copy-start(f32[8]{0:T(128)S(1)} %exp.158) | copy-start | bytes 100
  22.9 29.2 %copy-start.88 = (f32[4,1,256]{2,1,0:T(1,128)}, f32[4,1,256]{2,1,0:T(1,128)S(1)}, u32[]{:S(2)}) copy-start(f32[4,1,256]{2,1,0:T(1,128)S(1)} %convert_element_type.244) | copy-start | bytes 12292
  36.6 15.6 copy-start.97
  36.6 17.4 copy-start.108
  51.0 18.9 copy-start.91
  52.2 17.7 copy-start.57
  53.9 16.0 copy-start.39
  69.9 136.1 %copy-start.66 = (f32[1,4096]{1,0:T(1,128)}, f32[1,4096]{1,0:T(1,128)S(1)}, u32[]{:S(2)}) copy-start(f32[1,4096]{1,0:T(1,128)S(1)} %get-tuple-element.1577) | copy-start | bytes 49156
  73.2 132.8 %copy-start.23 = (f32[512,1024]{1,0:T(8,128)}, f32[512,1024]{1,0:T(8,128)S(1)}, u32[]{:S(2)}) copy-start(f32[512,1024]{1,0:T(8,128)S(1)} %fusion.204) | copy-start | bytes 6291460
  194.2 5.8 collective-permute-start
  566.5 13.4 copy-start.10
  649.6 15.0 copy-start.131
  650.5 126.9 %all-gather.34.cloned.1.call-start = ((), (), s32[]{:S(2)}) async-start(), calls=%async_computation.27 | async-start | bytes 5242880 | tf_op jit(solution)/shard_map/all_gather | solution.py:25
  651.0 254.6 %all-gather.24.cloned.1.call-start = ((), (), s32[]{:S(2)}) async-start(), calls=%async_computation.13 | async-start | bytes 5242880 | tf_op jit(solution)/shard_map/all_gather | solution.py:202
  651.6 287.3 %all-gather.26.cloned.1.call-start = ((), (), s32[]{:S(2)}) async-start(), calls=%async_computation.14 | async-start | bytes 5242880 | tf_op jit(solution)/shard_map/all_gather | solution.py:207
  652.4 373.4 %all-gather.28.cloned.1.call-start = ((), (), s32[]{:S(2)}) async-start(), calls=%async_computation.15 | async-start | bytes 5242880 | tf_op jit(solution)/shard_map/all_gather | solution.py:300
  946.3 160.9 %all-gather.30.cloned.1.call-start = ((), (), s32[]{:S(2)}) async-start(), calls=%async_computation.17 | async-start | bytes 5242880 | tf_op jit(solution)/shard_map/all_gather | solution.py:314
  948.8 321.4 %reduce-scatter.15.cloned.1.call-start = ((), (), s32[]{:S(2)}) async-start(), calls=%async_computation.18 | async-start | bytes 10485760 | tf_op jit(solution)/shard_map/reduce_scatter | solution.py:321
  1127.1 223.0 %reduce-scatter.13.cloned.1.call-start = ((), (), s32[]{:S(2)}) async-start(), calls=%async_computation.16 | async-start | bytes 5242880 | tf_op jit(solution)/shard_map/reduce_scatter | solution.py:305
  1134.3 332.8 %all-gather.36.cloned.1.call-start = ((), (), s32[]{:S(2)}) async-start(), calls=%async_computation.28 | async-start | bytes 2621440 | tf_op jit(solution)/shard_map/all_gather | solution.py:25
  1136.4 136.5 %copy-start.112 = (f32[512]{0:T(512)S(1)}, f32[512]{0:T(512)}, u32[]{:S(2)}) copy-start(f32[512]{0:T(512)} %copy-done.111) | copy-start | bytes 6148
  1136.4 213.7 %copy-start.43 = (bf16[512,1024]{1,0:T(8,128)(2,1)S(1)}, bf16[512,1024]{1,0:T(8,128)(2,1)}, u32[]{:S(2)}) copy-start(bf16[512,1024]{1,0:T(8,128)(2,1)} %param.38) | copy-start | bytes 3145732
  1136.4 403.9 %all-gather.38.cloned.1.call-start = ((), (), s32[]{:S(2)}) async-start(), calls=%async_computation.29 | async-start | bytes 5242880 | tf_op jit(solution)/shard_map/all_gather | solution.py:25
  1272.9 81.0 %copy-start.115 = (f32[1,2,8,128]{3,1,2,0:T(2,128)S(1)}, f32[1,2,8,128]{3,1,2,0:T(2,128)}, u32[]{:S(2)}) copy-start(f32[1,2,8,128]{3,1,2,0:T(2,128)} %copy.419) | copy-start | bytes 24580
  1368.9 90.1 %copy-start.99 = (f32[512]{0:T(512)S(1)}, f32[512]{0:T(512)}, u32[]{:S(2)}) copy-start(f32[512]{0:T(512)} %copy-done.97) | copy-start | bytes 6148
  1458.7 456.0 %reduce-scatter.23.cloned.1.call-start = ((), (), s32[]{:S(2)}) async-start(), calls=%async_computation.22 | async-start | bytes 5242880 | tf_op jit(solution)/shard_map/reduce_scatter | solution.py:405
  1465.5 449.2 %reduce-scatter.29.cloned.1.call-start = ((), (), s32[]{:S(2)}) async-start(), calls=%async_computation.25 | async-start | bytes 5242880 | tf_op jit(solution)/shard_map/reduce_scatter | solution.py:429
  1476.5 444.8 %reduce-scatter.17.cloned.1.call-start = ((), (), s32[]{:S(2)}) async-start(), calls=%async_computation.19 | async-start | bytes 2621440 | tf_op jit(solution)/shard_map/reduce_scatter | solution.py:387
  1819.6 12.8 copy-start.67
  1859.6 5.8 collective-permute-start.1
  1876.2 90.9 %reduce-scatter.19.cloned.1.call-start = ((), (), s32[]{:S(2)}) async-start(), calls=%async_computation.20 | async-start | bytes 2621440 | tf_op jit(solution)/shard_map/reduce_scatter | solution.py:393
  1880.2 165.3 %reduce-scatter.21.cloned.1.call-start = ((), (), s32[]{:S(2)}) async-start(), calls=%async_computation.21 | async-start | bytes 5242880 | tf_op jit(solution)/shard_map/reduce_scatter | solution.py:399
  1886.4 233.8 %reduce-scatter.31.cloned.1.call-start = ((), (), s32[]{:S(2)}) async-start(), calls=%async_computation.30 | async-start | bytes 1310720
  1905.4 215.8 %reduce-scatter.25.cloned.1.call-start = ((), (), s32[]{:S(2)}) async-start(), calls=%async_computation.23 | async-start | bytes 20480 | tf_op jit(solution)/shard_map/reduce_scatter | solution.py:411
  1906.0 215.3 %reduce-scatter.27.cloned.1.call-start = ((), (), s32[]{:S(2)}) async-start(), calls=%async_computation.24 | async-start | bytes 20480 | tf_op jit(solution)/shard_map/reduce_scatter | solution.py:417
  1907.4 345.4 %all-reduce.23.cloned.1.call-start = ((), (), s32[]{:S(2)}) async-start(), calls=%async_computation.31 | async-start | bytes 17039360 | tf_op jit(solution)/shard_map/psum | solution.py:438
  2046.9 48.1 %copy-start.83 = (bf16[1024,8]{0,1:T(8,128)(2,1)S(1)}, bf16[1024,8]{0,1:T(8,128)(2,1)}, u32[]{:S(2)}) copy-start(bf16[1024,8]{0,1:T(8,128)(2,1)} %copy-done.82) | copy-start | bytes 49156
  2053.4 42.6 %copy-start.85 = (bf16[1024,8]{0,1:T(8,128)(2,1)S(1)}, bf16[1024,8]{0,1:T(8,128)(2,1)}, u32[]{:S(2)}) copy-start(bf16[1024,8]{0,1:T(8,128)(2,1)} %copy-done.84) | copy-start | bytes 49156
  2103.1 13.6 copy-start.102
  (166 other events, 632.1 us)
Sparse Core Ops, SparseCore 0:
  9.7 49.3 all-gather.19
  60.6 44.7 all-gather.17
  106.9 79.4 all-gather.21
  650.6 45.2 all-gather.31
  697.9 79.3 all-gather.33
  778.7 79.2 all-gather.23
  859.6 79.2 all-gather.25
  946.4 79.2 all-gather.27
  1027.9 79.2 all-gather.29
  1127.2 142.9 reduce-scatter.14
  1272.5 77.4 reduce-scatter.12
  1352.1 46.4 all-gather.35
  1458.9 81.3 all-gather.37
  1542.5 75.2 reduce-scatter.22
  1620.0 77.2 reduce-scatter.28
  1876.4 44.8 reduce-scatter.16
  1923.9 43.1 reduce-scatter.18
  1969.4 76.0 reduce-scatter.20
  2048.4 27.8 reduce-scatter.30
  2079.0 17.7 reduce-scatter.24
  2099.6 17.0 reduce-scatter.26
  2123.9 128.8 all-reduce.22
where the time goes:
time: 2290 us; the launch traced here: 2270 us
  waiting for transfers between devices  889 us (39%)
  matrix products  503 us (22%)
  other arithmetic  470 us (21%)
  local copies, waits for them, and re-layouts  237 us (10%)
  blocking collectives  147 us (6%)
    another operation x4, other arithmetic, block_parts(): jax.scipy.linalg.solve_triangular(system, (betas_b * jnp.exp(cum_log))[.....  319 us
    all_gather x4, waiting for transfers between devices, carried_in(): pieces = jax.tree.map(lambda part: lax.all_gather(part, axis), value)  159 us
    dot_general x26, matrix products, matmul_low(): return jnp.dot(left, right, preferred_element_type=jnp.float32)  136 us
    reduce_scatter x1, waiting for transfers between devices, on_device(): lax.psum_scatter(matmul_low(gate_low, w_ffgate.T) + matmul_low(up_low, w_...  134 us
    psum x1, waiting for transfers between devices, on_device(): lax.psum(shards[1].astype(jnp.bfloat16), 'rep').astype(jnp.float32)  104 us
    squeeze x80, local copies, waits for them, and re-layouts, device_map(): lax.scan(compose, initial, (cum_log, wy_keys, wy_values, key_tilde))  84.5 us
    reduce_scatter x1, waiting for transfers between devices, on_device(): lax.psum_scatter(matmul_low(normed.T, value_low).astype(jnp.bfloat16), 'f...  78.4 us
    reduce_scatter x1, waiting for transfers between devices, on_device(): lax.psum_scatter(matmul_low(swiglu_out, w_ffdown).astype(jnp.bfloat16), '...  77.1 us
  transfers between devices with their start and end apart: 24, of which 15 were waited for; matrix products, arithmetic and copies ran while one was open for 31% of the time, Pallas kernels for 0%

commit v1 on v0

v1 whole, which is shorter than its diff:
```python
import functools

import jax
import jax.numpy as jnp
from jax import lax
from jax.experimental import pallas as pl
from jax.experimental.pallas import tpu as pltpu
from jax.sharding import PartitionSpec as P

DK = 128
DV = 256
KW = 4
CHUNK = 128
PAD = 16
VMEM_LIMIT = 56 * 1024 * 1024

norm_epsilon = 1e-06
head_epsilon = 1e-05
highest = lax.Precision.HIGHEST
f32 = jnp.float32
bf16 = jnp.bfloat16


MM, MM_T, T_MM = ((1,), (0,)), ((1,), (1,)), ((0,), (0,))


def low_dot(a, b, dims):
    return lax.dot_general(a.astype(bf16), b.astype(bf16), (dims, ((), ())), preferred_element_type=f32)


def fine_dot(a, b, dims):
    a_high, b_high = a.astype(bf16), b.astype(bf16)
    a_low = (a - a_high.astype(f32)).astype(bf16)
    b_low = (b - b_high.astype(f32)).astype(bf16)
    return (
        low_dot(a_high, b_high, dims) + low_dot(a_high, b_low, dims) + low_dot(a_low, b_high, dims)
    )


def mm(a, b):
    return low_dot(a, b, MM)


def mm_t(a, b):
    return low_dot(a, b, MM_T)


def t_mm(a, b):
    return low_dot(a, b, T_MM)


def places():
    rows = lax.broadcasted_iota(jnp.int32, (CHUNK, CHUNK), 0)
    cols = lax.broadcasted_iota(jnp.int32, (CHUNK, CHUNK), 1)
    return rows, cols


def unit_lower_inverses(lows, rows, cols):
    differ = rows ^ cols
    eye = jnp.where(rows == cols, 1.0, 0.0)
    inverses = [eye - jnp.where(differ == 1, low, 0.0) for low in lows]
    size = 2
    while size < CHUNK:
        off = (differ >= size) & (differ < 2 * size)
        inner = [fine_dot(jnp.where(off, low, 0.0), inv, MM) for low, inv in zip(lows, inverses)]
        inverses = [inv - fine_dot(inv, part, MM) for inv, part in zip(inverses, inner)]
        size *= 2
    return inverses


def convolve(ext_ref, taps_ref, count):
    total = taps_ref[0:1, :] * ext_ref[PAD - KW + 1 : PAD - KW + 1 + count, :]
    for j in range(1, KW):
        start = PAD - KW + 1 + j
        total = total + taps_ref[j : j + 1, :] * ext_ref[start : start + count, :]
    return total


def sigmoid(z):
    return 1.0 / (1.0 + jnp.exp(-z))


def chunk_decay(col_ref, row_ref, part, rows, cols):
    beta = col_ref[0, part, 0:1]
    cum = col_ref[0, part, 1:2]
    gap = cum - row_ref[0, :, part]
    decay = jnp.where(rows >= cols, jnp.exp(jnp.minimum(gap, 0.0)), 0.0)
    last = cum[CHUNK - 1 : CHUNK, :]
    return beta, cum, decay, last


def front_kernel(
    xq, xk, xv, cq, ck, cv, col_ref, row_ref,
    q_out, k_out, inv_out, w_out, u_out, a_out, m_out, map_out, end_out,
):
    count = q_out.shape[0]
    rows, cols = places()
    eye = jnp.where(rows == cols, 1.0, 0.0)
    act = convolve(xq, cq, count)
    act = act * sigmoid(act)
    q_out[...] = act * lax.rsqrt(jnp.sum(act * act, -1, keepdims=True) + norm_epsilon) * DK ** (-0.5)
    act = convolve(xk, ck, count)
    act = act * sigmoid(act)
    k_out[...] = act * lax.rsqrt(jnp.sum(act * act, -1, keepdims=True) + norm_epsilon)
    act = convolve(xv, cv, count)
    values = act * sigmoid(act)
    blocks = range(count // CHUNK)
    parts = [slice(b * CHUNK, (b + 1) * CHUNK) for b in blocks]
    gates = [chunk_decay(col_ref, row_ref, part, rows, cols) for part in parts]
    keys = [k_out[part, :] for part in parts]
    lows = [
        beta * fine_dot(key, key, MM_T) * jnp.where(rows > cols, decay, 0.0)
        for key, (beta, _, decay, _) in zip(keys, gates)
    ]
    inverses = unit_lower_inverses(lows, rows, cols)
    steps, offsets = [], []
    for b, part, key, inverse, (beta, cum, decay, last) in zip(blocks, parts, keys, inverses, gates):
        inv_out[0, b] = inverse
        wkey = fine_dot(inverse, beta * jnp.exp(cum) * key, MM)
        wval = fine_dot(inverse, beta * values[part, :], MM)
        w_out[part, :] = wkey
        u_out[part, :] = wval
        a_out[0, b] = mm_t(q_out[part, :], key) * decay
        tilde = jnp.exp(last - cum) * key
        step = jnp.exp(last) * eye - t_mm(tilde, wkey)
        m_out[0, b] = step
        steps.append(step)
        offsets.append(t_mm(tilde, wval))
    transit, offset = eye, jnp.zeros((DK, DV), f32)
    for b in blocks:
        map_out[0, b, :, :DK] = transit
        map_out[0, b, :, DK:] = offset
        if b == 0:
            transit, offset = steps[0], offsets[0]
        else:
            transit, offset = fine_dot(steps[b], transit, MM), fine_dot(steps[b], offset, MM) + offsets[b]
    end_out[0, :, :DK] = transit
    end_out[0, :, DK:] = offset


def output_kernel(
    q_ref, map_ref, start_ref, w_ref, u_ref, a_ref, col_ref, gate_ref, gain_ref,
    mixed_out, state_out, fresh_out, gated_out,
):
    count = q_ref.shape[0]
    start = start_ref[0].astype(f32)
    for b in range(count // CHUNK):
        part = slice(b * CHUNK, (b + 1) * CHUNK)
        state = start if b == 0 else fine_dot(map_ref[0, b, :, :DK], start, MM)
        state = state + map_ref[0, b, :, DK:]
        state_out[0, b] = state
        fresh = u_ref[part, :] - fine_dot(w_ref[part, :], state, MM)
        fresh_out[part, :] = fresh
        cum = col_ref[0, part, 1:2]
        mixed_out[part, :] = mm(jnp.exp(cum) * q_ref[part, :], state) + mm(a_ref[0, b], fresh)
    mixed = mixed_out[...]
    gate = gate_ref[...]
    scale = lax.rsqrt(jnp.mean(mixed * mixed, -1, keepdims=True) + head_epsilon)
    gated = mixed * scale * gain_ref[...] * (gate * sigmoid(gate))
    gated_out[...] = gated.astype(bf16)


def tail_back_kernel(
    dgated_ref, mixed_ref, gate_ref, gain_ref, q_ref, a_ref, w_ref, m_ref, col_ref,
    dgate_out, dmixed_out, into_out, own_out, dgain_out,
):
    count = q_ref.shape[0]
    dgated = dgated_ref[...]
    mixed = mixed_ref[...]
    gate = gate_ref[...]
    gain = gain_ref[...]
    sig = sigmoid(gate)
    scale = lax.rsqrt(jnp.mean(mixed * mixed, -1, keepdims=True) + head_epsilon)
    unit = mixed * scale
    dgate = dgated * unit * gain * (sig * (1.0 + gate * (1.0 - sig)))
    dgate_out[...] = dgate.astype(bf16)
    dy = dgated * (gate * sig)
    dgain_out[0] = jnp.sum(dy * unit, 0, keepdims=True)
    dy = dy * gain
    dmixed_out[...] = scale * (dy - unit * jnp.mean(dy * unit, -1, keepdims=True))
    blocks = count // CHUNK
    for b in range(blocks):
        part = slice(b * CHUNK, (b + 1) * CHUNK)
        cum = col_ref[0, part, 1:2]
        reach = jnp.exp(cum) * q_ref[part, :] - mm(a_ref[0, b], w_ref[part, :])
        into_out[0, b] = t_mm(reach, dmixed_out[part, :])
    carried = into_out[0, blocks - 1]
    for b in reversed(range(blocks - 1)):
        carried = fine_dot(m_ref[0, b], carried, T_MM) + into_out[0, b]
    own_out[0] = carried


def conv_back(dact, ext_ref, taps_ref, pad_ref, dext_out, dtaps_out, count):
    width = dact.shape[1]
    conv = convolve(ext_ref, taps_ref, count)
    sig = sigmoid(conv)
    dconv = dact * (sig * (1.0 + conv * (1.0 - sig)))
    pad_ref[0:PAD, :width] = jnp.zeros((PAD, width), f32)
    pad_ref[PAD : PAD + count, :width] = dconv
    pad_ref[PAD + count : PAD + count + 8, :width] = jnp.zeros((8, width), f32)
    total = None
    for j in range(KW):
        term = taps_ref[j : j + 1, :] * pad_ref[KW - 1 - j : KW - 1 - j + PAD + count, :width]
        total = term if total is None else total + term
        start = PAD - KW + 1 + j
        dtaps_out[j : j + 1, :] = jnp.sum(dconv * ext_ref[start : start + count, :], 0, keepdims=True)
    dext_out[...] = total.astype(bf16)


def back_kernel(
    xq, xk, xv, cq, ck, cv, col_ref, row_ref, end_ref, m_ref, into_ref, inv_ref, w_ref, u_ref, a_ref,
    state_ref, fresh_ref, dmixed_ref, q_ref, k_ref,
    dxq, dxk, dxv, dcq, dck, dcv, dcol_out, drow_out,
    dq_ref, dk_ref, dv_ref, pad_ref,
):
    count = q_ref.shape[0]
    rows, cols = places()
    act = convolve(xv, cv, count)
    dv_ref[...] = act * sigmoid(act)
    blocks = count // CHUNK
    ends = [end_ref[0].astype(f32)]
    for b in reversed(range(1, blocks)):
        ends.append(fine_dot(m_ref[0, b], ends[-1], T_MM) + into_ref[0, b])
    ends.reverse()
    is_last = lax.broadcasted_iota(jnp.int32, (CHUNK, 1), 0) == CHUNK - 1
    for b in range(blocks):
        part = slice(b * CHUNK, (b + 1) * CHUNK)
        carried = ends[b]
        beta, cum, decay, last = chunk_decay(col_ref, row_ref, part, rows, cols)
        strict = jnp.where(rows > cols, decay, 0.0)
        key = k_ref[part, :]
        query = q_ref[part, :]
        value = dv_ref[part, :]
        dmixed = dmixed_ref[part, :]
        fresh = fresh_ref[part, :]
        state = state_ref[0, b]
        scores = a_ref[0, b]
        grown = jnp.exp(cum)
        fade = jnp.exp(last - cum)
        tilde = fade * key
        dfresh = t_mm(scores, dmixed) + mm(tilde, carried)
        dscores = mm_t(dmixed, fresh)
        dreach = mm_t(dmixed, state)
        dquery = grown * dreach
        dcum = jnp.sum(dquery * query, -1, keepdims=True)
        gap = dscores * scores
        dinner = dscores * decay
        dq_ref[part, :] = dquery + mm(dinner, key)
        dkey = t_mm(dinner, query)
        dtilde = mm_t(fresh, carried)
        faded = jnp.sum(dtilde * tilde, -1, keepdims=True)
        dkey = dkey + fade * dtilde
        dcum = dcum - faded
        dlast = jnp.sum(faded, 0, keepdims=True) + jnp.exp(last) * jnp.sum(
            jnp.sum(state * carried, -1, keepdims=True), 0, keepdims=True
        )
        dwkey = -mm_t(dfresh, state)
        inverse = inv_ref[0, b]
        dbkey = t_mm(inverse, dwkey)
        dbval = t_mm(inverse, dfresh)
        along = jnp.sum(dbkey * key, -1, keepdims=True) * grown
        dbeta = along + jnp.sum(dbval * value, -1, keepdims=True)
        dcum = dcum + along * beta
        dkey = dkey + (beta * grown) * dbkey
        dv_ref[part, :] = beta * dbval
        dlow = -(mm_t(dbkey, w_ref[part, :]) + mm_t(dbval, u_ref[part, :])) * strict
        inner = mm_t(key, key)
        dbeta = dbeta + jnp.sum(dlow * inner, -1, keepdims=True)
        dlow = dlow * beta
        gap = gap + dlow * inner
        dkey = dkey + mm(dlow, key) + t_mm(dlow, key)
        dk_ref[part, :] = dkey
        dcum = dcum + jnp.sum(gap, -1, keepdims=True) + jnp.where(is_last, dlast, 0.0)
        dcol_out[0, part, 0:1] = dbeta
        dcol_out[0, part, 1:2] = dcum
        drow_out[0, :, part] = -jnp.sum(gap, 0, keepdims=True)
    for ext, taps, d_ref, dext, dtaps, factor in (
        (xq, cq, dq_ref, dxq, dcq, DK ** (-0.5)),
        (xk, ck, dk_ref, dxk, dck, 1.0),
    ):
        act = convolve(ext, taps, count)
        act = act * sigmoid(act)
        scale = lax.rsqrt(jnp.sum(act * act, -1, keepdims=True) + norm_epsilon)
        unit = act * scale
        dunit = d_ref[...] * factor
        dact = scale * (dunit - unit * jnp.sum(unit * dunit, -1, keepdims=True))
        conv_back(dact, ext, taps, pad_ref, dext, dtaps, count)
    conv_back(dv_ref[...], xv, cv, pad_ref, dxv, dcv, count)


class HeadCalls:
    def __init__(self, count, heads):
        self.count, self.heads, self.blocks = count, heads, count // CHUNK
        self.params = pltpu.CompilerParams(
            vmem_limit_bytes=VMEM_LIMIT, dimension_semantics=("arbitrary",)
        )
        h = heads
        ext = count + PAD
        self.ext_specs = [
            pl.BlockSpec((ext, DK), lambda i: (0, i)),
            pl.BlockSpec((ext, DK), lambda i: (0, i + h)),
            pl.BlockSpec((ext, DV), lambda i: (0, i + h)),
        ]
        self.tap_specs = [
            pl.BlockSpec((KW, DK), lambda i: (0, i)),
            pl.BlockSpec((KW, DK), lambda i: (0, i + h)),
            pl.BlockSpec((KW, DV), lambda i: (0, i + h)),
        ]
        self.col = pl.BlockSpec((1, count, 2), lambda i: (i, 0, 0))
        self.row = pl.BlockSpec((1, 1, count), lambda i: (i, 0, 0))
        self.gain = pl.BlockSpec((1, DV), lambda i: (0, 0))

    def wide(self, width):
        return pl.BlockSpec((self.count, width), lambda i: (0, i))

    def stack(self, *shape):
        return pl.BlockSpec((1,) + shape, lambda i: (i,) + (0,) * len(shape))

    def wide_shape(self, width, dtype=f32):
        return jax.ShapeDtypeStruct((self.count, self.heads * width), dtype)

    def stack_shape(self, *shape, dtype=f32):
        return jax.ShapeDtypeStruct((self.heads,) + shape, dtype)

    def call(self, kernel, in_specs, out_specs, out_shape, name, scratch=()):
        return pl.pallas_call(
            kernel,
            grid=(self.heads,),
            in_specs=in_specs,
            out_specs=out_specs,
            out_shape=out_shape,
            scratch_shapes=list(scratch),
            compiler_params=self.params,
            name=name,
        )

    def front(self, ext, taps, col, row):
        nb = self.blocks
        return self.call(
            front_kernel,
            self.ext_specs + self.tap_specs + [self.col, self.row],
            [
                self.wide(DK), self.wide(DK), self.stack(nb, CHUNK, CHUNK), self.wide(DK), self.wide(DV),
                self.stack(nb, CHUNK, CHUNK), self.stack(nb, DK, DK), self.stack(nb, DK, DK + DV),
                self.stack(DK, DK + DV),
            ],
            [
                self.wide_shape(DK), self.wide_shape(DK), self.stack_shape(nb, CHUNK, CHUNK),
                self.wide_shape(DK), self.wide_shape(DV), self.stack_shape(nb, CHUNK, CHUNK),
                self.stack_shape(nb, DK, DK), self.stack_shape(nb, DK, DK + DV),
                self.stack_shape(DK, DK + DV),
            ],
            "delta_front",
        )(ext, ext, ext, taps, taps, taps, col, row)

    def outputs(self, query, maps, start, wkey, wval, scores, col, gate_pre, gain):
        nb = self.blocks
        return self.call(
            output_kernel,
            [
                self.wide(DK), self.stack(nb, DK, DK + DV), self.stack(DK, DV), self.wide(DK), self.wide(DV),
                self.stack(nb, CHUNK, CHUNK), self.col, self.wide(DV), self.gain,
            ],
            [self.wide(DV), self.stack(nb, DK, DV), self.wide(DV), self.wide(DV)],
            [
                self.wide_shape(DV), self.stack_shape(nb, DK, DV), self.wide_shape(DV),
                self.wide_shape(DV, bf16),
            ],
            "delta_outputs",
        )(query, maps, start, wkey, wval, scores, col, gate_pre, gain)

    def tail_back(self, dgated, mixed, gate_pre, gain, query, scores, wkey, steps, col):
        nb = self.blocks
        return self.call(
            tail_back_kernel,
            [
                self.wide(DV), self.wide(DV), self.wide(DV), self.gain, self.wide(DK),
                self.stack(nb, CHUNK, CHUNK), self.wide(DK), self.stack(nb, DK, DK), self.col,
            ],
            [
                self.wide(DV), self.wide(DV), self.stack(nb, DK, DV), self.stack(DK, DV),
                self.stack(1, DV),
            ],
            [
                self.wide_shape(DV, bf16), self.wide_shape(DV), self.stack_shape(nb, DK, DV),
                self.stack_shape(DK, DV), self.stack_shape(1, DV),
            ],
            "delta_tail_back",
        )(dgated, mixed, gate_pre, gain, query, scores, wkey, steps, col)

    def back(self, ext, taps, col, row, end, steps, into, inverse, wkey, wval, scores, states, fresh, dmixed, query, key):
        nb, count, heads = self.blocks, self.count, self.heads
        rows = count + PAD
        square = self.stack(nb, CHUNK, CHUNK)
        return self.call(
            back_kernel,
            self.ext_specs + self.tap_specs + [
                self.col, self.row, self.stack(DK, DV), self.stack(nb, DK, DK), self.stack(nb, DK, DV),
                square, self.wide(DK), self.wide(DV), square, self.stack(nb, DK, DV), self.wide(DV),
                self.wide(DV), self.wide(DK), self.wide(DK),
            ],
            [
                pl.BlockSpec((rows, DK), lambda i: (0, i)), pl.BlockSpec((rows, DK), lambda i: (0, i)),
                pl.BlockSpec((rows, DV), lambda i: (0, i)), pl.BlockSpec((KW, DK), lambda i: (0, i)),
                pl.BlockSpec((KW, DK), lambda i: (0, i)), pl.BlockSpec((KW, DV), lambda i: (0, i)),
                self.col, self.row,
            ],
            [
                jax.ShapeDtypeStruct((rows, heads * DK), bf16), jax.ShapeDtypeStruct((rows, heads * DK), bf16),
                jax.ShapeDtypeStruct((rows, heads * DV), bf16), jax.ShapeDtypeStruct((KW, heads * DK), f32),
                jax.ShapeDtypeStruct((KW, heads * DK), f32), jax.ShapeDtypeStruct((KW, heads * DV), f32),
                jax.ShapeDtypeStruct((heads, count, 2), f32), jax.ShapeDtypeStruct((heads, 1, count), f32),
            ],
            "delta_back",
            [
                pltpu.VMEM((count, DK), f32), pltpu.VMEM((count, DK), f32), pltpu.VMEM((count, DV), f32),
                pltpu.VMEM((PAD + count + 8, DV), f32),
            ],
        )(
            ext, ext, ext, taps, taps, taps, col, row, end, steps, into, inverse, wkey, wval, scores,
            states, fresh, dmixed, query, key,
        )


def rep_piece(block, rows):
    return lax.dynamic_slice_in_dim(block, lax.axis_index("rep") * rows, rows, 0)


def gather_everywhere(block):
    return lax.all_gather(block, ("fsdp", "rep"), axis=0, tiled=True)


def passed_along(block, distance):
    devices = range(lax.axis_size("fsdp"))
    route = [(i - distance, i) for i in devices if i - distance in devices]
    return lax.ppermute(block, "fsdp", route)


def carried_states(transit, offset, backward):
    count = lax.axis_size("fsdp")
    carried = jnp.zeros_like(offset)
    for hop in range(count - 1):
        source = count - 1 - hop if backward else hop
        target = source - 1 if backward else source + 1
        moved = offset
        if hop:
            form = "hed,hef->hdf" if backward else "hde,hef->hdf"
            moved = moved + jnp.einsum(form, transit, carried, preferred_element_type=f32)
        arrived = lax.ppermute(moved.astype(bf16), "fsdp", [(source, target)])
        carried = carried + arrived.astype(f32)
    return carried


def partners(bit):
    return [(i, i ^ bit) for i in range(lax.axis_size("rep"))]


def halves(block, axis, bit):
    mine = (lax.axis_index("rep") // bit) % 2
    return (
        lax.dynamic_index_in_dim(block, mine, axis, keepdims=False),
        lax.dynamic_index_in_dim(block, 1 - mine, axis, keepdims=False),
    )


def halve(block, axis, bit):
    kept, sent = halves(block, axis, bit)
    return kept + lax.ppermute(sent, "rep", partners(bit))


def sum_to_owners(grads):
    owners, reps = lax.axis_size("fsdp"), lax.axis_size("rep")
    levels = reps.bit_length() - 1
    width = grads[0].shape[1]
    sizes = [grad.shape[0] // (owners * reps) for grad in grads]
    pairs = [
        halves(grad.reshape((owners,) + (2,) * levels + (size, width)), levels, 1)
        for grad, size in zip(grads, sizes)
    ]
    kept, sent = [jnp.concatenate(side, -2) for side in zip(*pairs)]
    block = kept + lax.ppermute(sent, "rep", partners(1))
    left = block[..., : width // 2]
    right = block[..., width // 2 :]
    for level in range(1, levels):
        left = halve(left, levels - level, 1 << level)
        right = halve(right, 1, 1 << (levels - level))
    block = jnp.concatenate([left, right], -1).reshape(-1, width)
    block = lax.psum_scatter(block, "fsdp", scatter_dimension=0, tiled=True)
    block = lax.all_gather(block, "rep", axis=0)
    sums, at = [], 0
    for size in sizes:
        sums.append(block[:, at : at + size].reshape(-1, width).astype(f32))
        at += size
    return sums


def sum_everywhere(block):
    for axis in ("rep", "fsdp"):
        size = lax.axis_size(axis)
        bit = 1
        while bit < size:
            block = block + lax.ppermute(block, axis, [(i, i ^ bit) for i in range(size)])
            bit *= 2
    return block


def matmul_low(left, right):
    return jnp.dot(left, right, preferred_element_type=f32)


def matmul_high(left, right):
    return jnp.dot(left, right, precision=highest, preferred_element_type=f32)


def matmul_nt(left, right):
    return lax.dot_general(left, right, (((1,), (1,)), ((), ())), preferred_element_type=f32)


def matmul_tn(left, right):
    return lax.dot_general(left, right, (((0,), (0,)), ((), ())), preferred_element_type=f32)


def rms_scale(values, gain):
    return values * lax.rsqrt(jnp.mean(values * values, -1, keepdims=True) + norm_epsilon) * gain


def swiglu(ff_gate, ff_up):
    return jax.nn.silu(ff_gate) * ff_up


def head_gates(beta_pre, decay_pre, a_log, dt_bias, valid_mask):
    row_count, head_count = beta_pre.shape
    beta_gate = valid_mask * jax.nn.sigmoid(beta_pre)
    log_decay = -valid_mask * jnp.exp(a_log) * jax.nn.softplus(decay_pre + dt_bias)
    cum_log = jnp.cumsum(log_decay.reshape(row_count // CHUNK, CHUNK, head_count), 1)
    return beta_gate, cum_log.reshape(row_count, head_count)


def on_device(
    tokens, cotangent, valid_count, norm_mix, w_query, w_key, w_value, w_gate, w_beta, w_decay,
    a_log, dt_bias, conv_weight, norm_head, w_out, norm_ffn, w_ffgate, w_ffup, w_ffdown,
):
    row_count, width = tokens.shape
    head_count = a_log.shape[0]
    owners, reps = lax.axis_size("fsdp"), lax.axis_size("rep")
    qk_width = head_count * DK
    own_count = valid_count[0, 0]
    valid_mask = (jnp.arange(row_count) < own_count).astype(f32)[:, None]

    share = w_query.shape[0] // reps
    w_qkv = gather_everywhere(
        jnp.concatenate([rep_piece(w, share) for w in (w_query, w_key, w_value)], 1)
    )
    gate_pieces = rep_piece(w_gate, share)
    parts = [
        gate_pieces[:, :width],
        gate_pieces[:, width:],
        rep_piece(w_out, w_out.shape[0] // reps),
        rep_piece(w_ffgate.T, w_ffgate.shape[1] // reps),
        rep_piece(w_ffup.T, w_ffup.shape[1] // reps),
        rep_piece(w_ffdown, w_ffdown.shape[0] // reps),
    ]
    packed, w_qkv = lax.optimization_barrier((jnp.concatenate(parts, 0), w_qkv))
    rest = gather_everywhere(packed).reshape(owners * reps, -1, width)
    whole, at = [], 0
    for part in parts:
        whole.append(rest[:, at : at + part.shape[0]].reshape(-1, width))
        at += part.shape[0]
    gate_left, gate_right, out_full, ffgate_t, ffup_t, ffdown_full = whole

    small = [norm_mix, norm_ffn, norm_head, w_beta.reshape(-1), w_decay.reshape(-1), conv_weight.reshape(-1)]
    small_full = lax.all_gather(jnp.concatenate(small), "fsdp", axis=0)
    at, pieces = 0, []
    for part in small:
        pieces.append(small_full[:, at : at + part.shape[0]])
        at += part.shape[0]
    mix_gain, ffn_gain, head_gain = [p.reshape(-1).astype(f32) for p in pieces[:3]]
    w_beta_decay = jnp.concatenate([p.reshape(width, head_count) for p in pieces[3:5]], 1)
    taps = pieces[5].reshape(owners, KW, -1).transpose(1, 0, 2).reshape(KW, -1).astype(f32)
    head_gain = head_gain[None, :]

    inputs = tokens.astype(f32)
    edge_place = own_count - (KW - 1)
    before = passed_along(lax.dynamic_slice_in_dim(tokens, edge_place, KW - 1, 0), 1)
    ahead = jnp.concatenate([jnp.zeros((PAD - KW + 1, width), f32), before.astype(f32)], 0)
    normed_f32, mix_pull = jax.vjp(rms_scale, inputs, mix_gain)
    normed = normed_f32.astype(bf16)
    normed_ext = jnp.concatenate([rms_scale(ahead, mix_gain).astype(bf16), normed], 0)
    projected = matmul_low(normed_ext, w_qkv)
    gates_pre = matmul_low(normed, w_beta_decay)
    beta_pre, decay_pre = gates_pre[:, :head_count], gates_pre[:, head_count:]
    (beta_gate, cum_log), gates_pull = jax.vjp(
        lambda *args: head_gates(*args, valid_mask), beta_pre, decay_pre, a_log, dt_bias
    )
    col = jnp.stack([beta_gate.T, cum_log.T], -1)
    row = cum_log.T[:, None, :]
    calls = HeadCalls(row_count, head_count)
    query, key, inverse, wkey, wval, scores, steps, maps, end_map = calls.front(projected, taps, col, row)
    transit = end_map[:, :, :DK]
    start_state = carried_states(transit, end_map[:, :, DK:], False)
    gate_pre = jnp.concatenate([matmul_low(normed, gate_left), matmul_low(normed, gate_right)], 1)
    mixed, states, fresh, gated_out = calls.outputs(
        query, maps, start_state, wkey, wval, scores, col, gate_pre, head_gain
    )
    residual = inputs + matmul_low(gated_out, out_full)

    ffn_f32, ffn_pull = jax.vjp(rms_scale, residual, ffn_gain)
    normed_ffn = ffn_f32.astype(bf16)
    swiglu_f32, swiglu_pull = jax.vjp(
        swiglu, matmul_nt(normed_ffn, ffgate_t), matmul_nt(normed_ffn, ffup_t)
    )
    swiglu_out = swiglu_f32.astype(bf16)
    output = (valid_mask * (residual + matmul_low(swiglu_out, ffdown_full))).astype(bf16)
    out_grad = cotangent.astype(f32) * valid_mask
    out_low = out_grad.astype(bf16)
    gate_grad_f32, up_grad_f32 = swiglu_pull(matmul_nt(out_low, ffdown_full))
    gate_low = gate_grad_f32.astype(bf16)
    up_low = up_grad_f32.astype(bf16)
    ffn_in_grad = matmul_low(gate_low, ffgate_t) + matmul_low(up_low, ffup_t)
    residual_part, ffn_gain_grad = ffn_pull(ffn_in_grad)
    residual_grad = out_grad + residual_part
    residual_low = residual_grad.astype(bf16)

    dgated = matmul_nt(residual_low, out_full)
    dgate_low, dmixed, into, own_grad, dgain = calls.tail_back(
        dgated, mixed, gate_pre, head_gain, query, scores, wkey, steps, col
    )
    end_grad = carried_states(transit, own_grad, True)

    ffdown_grad, ffgate_grad, ffup_grad = sum_to_owners([
        matmul_tn(swiglu_out, out_low).astype(bf16),
        matmul_tn(gate_low, normed_ffn).astype(bf16),
        matmul_tn(up_low, normed_ffn).astype(bf16),
    ])
    out_weight_grad, gate_left_grad, gate_right_grad = sum_to_owners([
        matmul_tn(gated_out, residual_low).astype(bf16),
        matmul_tn(normed, dgate_low[:, :width]).astype(bf16),
        matmul_tn(normed, dgate_low[:, width:]).astype(bf16),
    ])

    dxq, dxk, dxv, dtap_q, dtap_k, dtap_v, dcol, drow = calls.back(
        projected, taps, col, row, end_grad, steps, into, inverse, wkey, wval, scores, states, fresh,
        dmixed, query, key,
    )
    dprojected = jnp.concatenate([dxq, dxk, dxv], 1)
    (qkv_grad,) = sum_to_owners([matmul_tn(normed_ext, dprojected).astype(bf16)])
    coming = passed_along(dprojected[PAD - KW + 1 : PAD], -1)
    own_low = dprojected[PAD:]
    edge_rows = lax.dynamic_slice_in_dim(own_low, edge_place, KW - 1, 0).astype(f32) + coming.astype(f32)
    own_low = lax.dynamic_update_slice_in_dim(own_low, edge_rows.astype(bf16), edge_place, 0)
    beta_pre_grad, decay_pre_grad, rate_grad, bias_grad = gates_pull(
        (dcol[:, :, 0].T, (dcol[:, :, 1] + drow[:, 0, :]).T)
    )
    gates_grad = jnp.concatenate([beta_pre_grad, decay_pre_grad], 1)
    normed_grad = (
        matmul_nt(own_low, w_qkv)
        + matmul_nt(dgate_low[:, :width], gate_left)
        + matmul_nt(dgate_low[:, width:], gate_right)
        + matmul_high(gates_grad, w_beta_decay.astype(f32).T)
    )
    input_part, mix_gain_grad = mix_pull(normed_grad)
    grad_tokens = residual_grad + input_part

    gates_weight_grad = lax.dot_general(
        normed.astype(f32), gates_grad, (((0,), (0,)), ((), ())), precision=highest,
        preferred_element_type=f32,
    )
    dtaps = jnp.concatenate([dtap_q, dtap_k, dtap_v], 1)
    small = [
        mix_gain_grad, ffn_gain_grad, jnp.sum(dgain, 0).reshape(-1), gates_weight_grad.reshape(-1),
        dtaps.reshape(-1), rate_grad, bias_grad,
    ]
    flat = jnp.concatenate(small)
    lanes = 128
    flat = jnp.pad(flat, (0, -flat.shape[0] % (8 * lanes))).reshape(-1, lanes)
    sums = sum_everywhere(flat).reshape(-1)
    at, pieces = 0, []
    for part in small:
        pieces.append(sums[at : at + part.shape[0]])
        at += part.shape[0]
    mine = lax.axis_index("fsdp")

    def own(block, axis):
        size = block.shape[axis] // owners
        return lax.dynamic_slice_in_dim(block, mine * size, size, axis)

    gates_weight = own(pieces[3].reshape(width, 2 * head_count), 0)
    return (
        output,
        grad_tokens,
        own(pieces[0], 0),
        qkv_grad[:, :qk_width],
        qkv_grad[:, qk_width : 2 * qk_width],
        qkv_grad[:, 2 * qk_width :],
        jnp.concatenate([gate_left_grad, gate_right_grad], 1),
        gates_weight[:, :head_count],
        gates_weight[:, head_count:],
        pieces[5],
        pieces[6],
        own(pieces[4].reshape(KW, -1), 1),
        own(pieces[2], 0),
        out_weight_grad,
        own(pieces[1], 0),
        ffgate_grad.T,
        ffup_grad.T,
        ffdown_grad,
    )


def solution(mesh):
    rows = P(("rep", "fsdp"), None)
    first, second, vector = P("fsdp", None), P(None, "fsdp"), P("fsdp")
    placed = (
        rows, rows, P("rep", "fsdp"), vector, first, first, first, first, first, first, P(), P(),
        second, vector, first, vector, second, second, first,
    )
    given = (
        rows, rows, vector, first, first, first, first, first, first, P(), P(), second, vector, first,
        vector, second, second, first,
    )
    return jax.shard_map(on_device, mesh=mesh, in_specs=placed, out_specs=given, check_vma=False)
```

time: 2290 us -> 845 us (0.37)
  waiting for transfers between devices: 889 us -> 374 us
  other arithmetic: 470 us -> 63 us
  matrix products: 503 us -> 114 us
  blocking collectives: 147 us -> 0 us
  local copies, waits for them, and re-layouts: 237 us -> 102 us
  Pallas kernels: 0 us -> 124 us
  starting transfers between devices: 5.61 us -> 37.8 us
    dot_general x257 -> x28, matrix products: 465 us -> 114 us  [the longest x7 44.6 us: matmul_nt(): lax.dot_general(left, right, (((1,), (1,)), ((), ())), preferred_element_...]
    another operation x14 -> x4, other arithmetic: 333 us -> 4.78 us  [the longest x2 4.69 us: head_gates(): jnp.cumsum(log_decay.reshape(row_count // CHUNK, CHUNK, head_count), 1)]
    reduce_scatter x9 -> x3, waiting for transfers between devices: 342 us -> 26 us  [sum_to_owners(): block = lax.psum_scatter(block, 'fsdp', scatter_dimension=0, tiled=True)]
    all_gather x11 -> x5, waiting for transfers between devices: 436 us -> 161 us  [the longest x2 136 us: gather_everywhere(): return lax.all_gather(block, ('fsdp', 'rep'), axis=0, tiled=True)]
    ppermute x2 -> x28, waiting for transfers between devices: 2.97 us -> 186 us  [the longest x12 124 us: halve(): return kept + lax.ppermute(sent, 'rep', partners(bit))]
    pallas_call x0 -> x4, Pallas kernels: none -> 124 us  [the longest x1 48 us: back(): self.call(back_kernel, self.ext_specs + self.tap_specs + [self.col, self....]
    psum x1 -> x0, waiting for transfers between devices: 104 us -> none  [on_device(): lax.psum(shards[1].astype(jnp.bfloat16), 'rep').astype(jnp.float32)]
    squeeze x88 -> x17, local copies, waits for them, and re-layouts: 95.2 us -> 17.3 us  [the longest x6 11.8 us: halves(): lax.dynamic_index_in_dim(block, mine, axis, keepdims=False)]
  transfers between devices with their start and end apart: 24 -> 37, of which waited for: 15 -> 18; matrix products, arithmetic and copies ran while one was open for 31% -> 22% of each run, Pallas kernels for 0% -> 11%
where the time goes in v1:
time: 845 us; the launch traced here: 834 us
  waiting for transfers between devices  374 us (44%)
  Pallas kernels  124 us (15%)
  matrix products  114 us (13%)
  local copies, waits for them, and re-layouts  102 us (12%)
  other arithmetic  63 us (7%)
  starting transfers between devices  37.8 us (4%)
  between operations  18.8 us (2%)
    all_gather x2, waiting for transfers between devices, gather_everywhere(): return lax.all_gather(block, ('fsdp', 'rep'), axis=0, tiled=True)  136 us
    ppermute x12, waiting for transfers between devices, halve(): return kept + lax.ppermute(sent, 'rep', partners(bit))  124 us
    pallas_call x1, Pallas kernels, back(): self.call(back_kernel, self.ext_specs + self.tap_specs + [self.col, self....  48 us
    ppermute x6, waiting for transfers between devices, carried_states(): arrived = lax.ppermute(moved.astype(bf16), 'fsdp', [(source, target)])  48 us
    dot_general x7, matrix products, matmul_nt(): lax.dot_general(left, right, (((1,), (1,)), ((), ())), preferred_element_...  44.6 us
    pallas_call x1, Pallas kernels, front(): self.call(front_kernel, self.ext_specs + self.tap_specs + [self.col, self...  40.9 us
    dot_general x8, matrix products, matmul_low(): return jnp.dot(left, right, preferred_element_type=f32)  37 us
    reduce_scatter x3, waiting for transfers between devices, sum_to_owners(): block = lax.psum_scatter(block, 'fsdp', scatter_dimension=0, tiled=True)  26 us
  transfers between devices with their start and end apart: 37, of which 18 were waited for; matrix products, arithmetic and copies ran while one was open for 22% of the time, Pallas kernels for 11%

profile of v1, /device:TPU:0, one launch (start us, length us, event | category | flops | bytes accessed | tf_op | source)
XLA Modules:
  0.0 834.2 jit_solution(5016748540407604459)
XLA Ops:
  24.2 68.7 %all-gather.10.cloned.1.call-done = bf16[1024,4096]{1,0:T(8,128)(2,1)} async-done(((bf16[32,4096]{1,0:T(8,128)(2,1)}), bf16[1024,4096]{1,0:T(8,128)(2,1)}) %all-gather.10.cloned.1.call-update) | async-done | bytes 8388624 | tf_op jit(solution)/shard_map/all_gather | solution.py:430
  93.6 3.4 collective-permute-start
  106.0 10.2 %fusion.23.xq.xk.xv = f32[528,4096]{1,0:T(8,128)} fusion(bf16[1024,4096]{1,0:T(8,128)(2,1)} %all-gather.10.cloned.1.call-done, bf16[512,1024]{1,0:T(8,128)(2,1)S(1)} %fusion.6, bf16[16,1024]{1,0:T(8,128)(2,1)S(1)} %fusion.36), kind=kOutput, calls=%fused_computation.102 | convolution fusion | flops 4431347712 | bytes 18120704 | tf_op jit(solution)/shard_map/dot_general | solution.py:508
  116.2 40.9 %delta_front.1 = (f32[512,1024]{1,0:T(8,128)}, f32[512,1024]{1,0:T(8,128)}, f32[8,4,128,128]{3,2,1,0:T(8,128)}, f32[512,1024]{1,0:T(8,128)}, f32[512,2048]{1,0:T...) custom-call(f32[528,4096]{1,0:T(8,128)} %fusion.23.xq.xk.xv, ...), custom_call_target="tpu_custom_call" | custom-call | tf_op jit(solution)/shard_map/delta_front/pallas_call | solution.py:339
  158.4 4.2 collective-permute-start.1
  162.6 16.7 %collective-permute-done.1 = bf16[8,128,256]{2,1,0:T(8,128)(2,1)S(1)} collective-permute-done((bf16[8,128,256]{2,1,0:T(8,128)(2,1)S(1)}, bf16[8,128,256]{2,1,0:T(8,128)(2,1)S(1)}, u32[]{:S(2)}, u32[]{:S(2)}) %collective-permute-start.1) | collective-permute-done | bytes 524320 | tf_op jit(solution)/shard_map/ppermute | solution.py:449
  189.0 67.5 %all-gather.12.cloned.1.call-done = bf16[12544,1024]{1,0:T(8,128)(2,1)} async-done(((bf16[392,1024]{1,0:T(8,128)(2,1)}), bf16[12544,1024]{1,0:T(8,128)(2,1)}) %all-gather.12.cloned.1.call-update) | async-done | bytes 25690128 | tf_op jit(solution)/shard_map/all_gather | solution.py:430
  256.5 4.9 slice.217
  261.4 2.7 fusion.68
  264.1 14.7 %fusion.67 = (bf16[32,88,1024]{2,1,0:T(8,128)(2,1)}, bf16[32,88,1024]{2,1,0:T(8,128)(2,1)}, bf16[32,88,1024]{2,1,0:T(8,128)(2,1)}) fusion(bf16[32,392,1024]{2,1,0:T(8,128)(2,1)} %bitcast.238), kind=kLoop, calls=%fused_computation.206 | loop fusion | bytes 34603008 | tf_op jit(solution)/shard_map/slice | solution.py:567
  283.9 18.3 %delta_outputs.1 = (f32[512,2048]{1,0:T(8,128)}, f32[8,4,128,256]{3,2,1,0:T(8,128)}, f32[512,2048]{1,0:T(8,128)}, bf16[512,2048]{1,0:T(8,128)(2,1)}) custom-call(f32[512,1024]{1,0:T(8,128)} %get-tuple-element.47.q_ref, f32[8,4,128,384]{3,2,1,0:T(8,128)} %get-tuple-element.48.map_ref, f32[8,128,256]{2,1,0:T(8,128)} %convert_add_fusion.3.start_ref, ...), custom_call_target="tpu_custom_call" | custom-call | tf_op jit(solution)/shard_map/delta_outputs/pallas_call | solution.py:358
  302.2 5.4 multiply_reduce_fusion.2
  308.0 5.0 fusion.82
  313.0 5.0 fusion.81
  318.0 10.5 %multiply_convert_fusion = (bf16[512,2816]{1,0:T(8,128)(2,1)}, bf16[512,2816]{1,0:T(8,128)(2,1)}, bf16[512,2816]{1,0:T(8,128)(2,1)}) fusion(f32[512,2816]{1,0:T(8,128)} %fusion.81, f32[512,2816]{1,0:T(8,128)} %fusion.82, bf16[2816,1024]{1,0:T(8,128)(2,1)S(1)} %bitcast.247, bf16[512,1024]{1,0:T(8,128)(2,1)S(1)} %copy-done.32, f32[512]{0:T(512)S(1)} %fusion.54), kind=kOutput, calls=%fused_computation.7 | convolution fusion | flops 2977431552 | bytes 27002880 | tf_op jit(solution)/shard_map/dot_general | solution.py:516
  328.6 6.3 fusion.83
  334.9 4.1 multiply_reduce_fusion
  341.2 4.4 fusion.25.dgated_ref
  345.6 16.5 %delta_tail_back.1 = (bf16[512,2048]{1,0:T(8,128)(2,1)}, f32[512,2048]{1,0:T(8,128)}, f32[8,4,128,256]{3,2,1,0:T(8,128)}, f32[8,128,256]{2,1,0:T(8,128)}, f32[8,1,256]{2,1,0:T(1,128)}) custom-call(f32[512,2048]{1,0:T(8,128)} %fusion.25.dgated_ref, f32[512,2048]{1,0:T(8,128)} %get-tuple-element.55.mixed_ref, f32[512,2048]{1,0:T(8,128)} %pad_maximum_fusion.1.gate_ref, ...), custom_call_target="tpu_custom_call" | custom-call | tf_op jit(solution)/shard_map/delta_tail_back/pallas_call | solution.py:374
  368.8 3.7 convolution_convert_fusion.1
  378.2 3.5 convolution_convert_fusion.3
  385.0 3.4 convolution_convert_fusion.2
  399.1 4.3 pad_maximum_fusion
  403.6 31.3 %collective-permute-done.6 = bf16[8,128,256]{2,1,0:T(8,128)(2,1)S(1)} collective-permute-done((bf16[8,128,256]{2,1,0:T(8,128)(2,1)S(1)}, bf16[8,128,256]{2,1,0:T(8,128)(2,1)S(1)}, u32[]{:S(2)}, u32[]{:S(2)}) %collective-permute-start.6) | collective-permute-done | bytes 524320 | tf_op jit(solution)/shard_map/ppermute | solution.py:449
  436.0 48.0 %delta_back.1 = (bf16[528,1024]{1,0:T(8,128)(2,1)}, bf16[528,1024]{1,0:T(8,128)(2,1)}, bf16[528,2048]{1,0:T(8,128)(2,1)}, f32[4,1024]{1,0:T(4,128)}, f32[4,1024]...) custom-call(f32[528,4096]{1,0:T(8,128)} %fusion.23.xq.xk.xv, ...), custom_call_target="tpu_custom_call" | custom-call | tf_op jit(solution)/shard_map/delta_back/pallas_call | solution.py:395
  487.1 7.0 convolution_convert_fusion
  494.1 2.9 constant_dynamic-slice_fusion.5
  499.5 5.5 maximum_add_fusion.1
  510.9 22.4 %collective-permute-done.21 = bf16[4,2,128,512]{3,2,1,0:T(8,128)(2,1)} collective-permute-done((bf16[4,2,128,512]{3,2,1,0:T(8,128)(2,1)}, bf16[4,2,128,512]{3,2,1,0:T(8,128)(2,1)}, u32[]{:S(2)}, u32[]{:S(2)}) %collective-permute-start.21) | collective-permute-done | bytes 1048608 | tf_op jit(solution)/shard_map/ppermute | solution.py:468
  536.1 2.8 bitcast_add_fusion
  545.7 4.0 collective-permute-done.22
  549.7 6.6 collective-permute-done.20
  557.6 13.1 %collective-permute-done.14 = bf16[4,2,32,2048]{3,2,1,0:T(8,128)(2,1)} collective-permute-done((bf16[4,2,32,2048]{3,2,1,0:T(8,128)(2,1)}, bf16[4,2,32,2048]{3,2,1,0:T(8,128)(2,1)}, u32[]{:S(2)}, u32[]{:S(2)}) %collective-permute-start.14) | collective-permute-done | bytes 1048608 | tf_op jit(solution)/shard_map/ppermute | solution.py:468
  573.8 7.5 maximum_add_fusion
  590.3 56.4 %collective-permute-done.17 = bf16[4,32,2048]{2,1,0:T(8,128)(2,1)S(1)} collective-permute-done((bf16[4,32,2048]{2,1,0:T(8,128)(2,1)S(1)}, bf16[4,32,2048]{2,1,0:T(8,128)(2,1)S(1)}, u32[]{:S(2)}, u32[]{:S(2)}) %collective-permute-start.17) | collective-permute-done | bytes 524320 | tf_op jit(solution)/shard_map/ppermute | solution.py:468
  655.4 17.6 %collective-permute-done.27 = bf16[4,264,512]{2,1,0:T(8,128)(2,1)S(1)} collective-permute-done((bf16[4,264,512]{2,1,0:T(8,128)(2,1)S(1)}, bf16[4,264,512]{2,1,0:T(8,128)(2,1)S(1)}, u32[]{:S(2)}, u32[]{:S(2)}) %collective-permute-start.27) | collective-permute-done | bytes 1081376 | tf_op jit(solution)/shard_map/ppermute | solution.py:468
  673.1 3.7 collective-permute-done.25
  680.4 4.2 fusion.18
  688.0 4.4 reduce_window_sum.23
  694.1 26.0 %reduce-scatter.8.cloned.1.call-done = bf16[264,1024]{1,0:T(8,128)(2,1)} async-done(((bf16[1056,1024]{1,0:T(8,128)(2,1)}), bf16[264,1024]{1,0:T(8,128)(2,1)}) %reduce-scatter.8.cloned.1.call-update) | async-done | bytes 540688 | tf_op jit(solution)/shard_map/reduce_scatter | solution.py:488
  725.0 4.8 slice.222
  732.4 12.9 %fusion.7 = (f32[1024]{0:T(1024)S(1)}, f32[512]{0:T(512)S(1)}, f32[512,1024]{1,0:T(8,128)}) fusion(bf16[512,1024]{1,0:T(8,128)(2,1)S(1)} %copy-done.7, f32[512]{0:T(512)S(1)} %copy-done.47, f32[1024]{0:T(1024)S(1)} %bitcast.285, f32[512,1024]{1,0:T(8,128)} %fusion.38, f32[512,1024]{1,0:T(8,128)} %fusion.18, f32[512,1024]{1,0:T(8,128)} %fusion.21, ...), kind=kOutput, calls=%fused_computation.43 | convolution fusion | flops 4300208640 | bytes 22032384 | tf_op jit(solution)/shard_map/dot_general | solution.py:516
  749.0 4.5 collective-permute-done.9
  756.2 8.0 multiply_convert_fusion.2
  767.0 3.1 collective-permute-done.11
  774.2 3.8 collective-permute-done.12
  788.0 3.1 slice.231
  792.6 25.0 %all-gather.18.cloned.1.call-done = bf16[2112,1024]{1,0:T(8,128)(2,1)} async-done(((bf16[264,1024]{1,0:T(8,128)(2,1)}), bf16[2112,1024]{1,0:T(8,128)(2,1)}) %all-gather.18.cloned.1.call-update) | async-done | bytes 4325392 | tf_op jit(solution)/shard_map/all_gather | solution.py:489
  (377 shorter events, 162.6 us)
Async XLA Ops:
  8.0 85.6 %copy-start.6 = (bf16[512,1024]{1,0:T(8,128)(2,1)S(1)}, bf16[512,1024]{1,0:T(8,128)(2,1)}, u32[]{:S(2)}) copy-start(bf16[512,1024]{1,0:T(8,128)(2,1)} %param.19) | copy-start | bytes 3145732
  8.1 84.8 %all-gather.10.cloned.1.call-start = ((), (), s32[]{:S(2)}) async-start(), calls=%async_computation.3 | async-start | bytes 8650752 | tf_op jit(solution)/shard_map/all_gather | solution.py:430
  10.9 86.5 %copy-start.64 = (f32[8]{0:T(128)S(1)}, f32[8]{0:T(128)}, u32[]{:S(2)}) copy-start(f32[8]{0:T(128)} %param.29) | copy-start | bytes 100
  10.9 87.6 %all-reduce.5.cloned.1.call-start = ((), (), s32[]{:S(2)}) async-start(), calls=%async_computation.11 | async-start | bytes 143360
  18.6 237.8 %all-gather.12.cloned.1.call-start = ((), (), s32[]{:S(2)}) async-start(), calls=%async_computation.4 | async-start | bytes 26492928 | tf_op jit(solution)/shard_map/all_gather | solution.py:430
  24.1 68.7 %copy-start.33 = (bf16[392,1024]{1,0:T(8,128)(2,1)}, bf16[392,1024]{1,0:T(8,128)(2,1)S(1)}, u32[]{:S(2)}) copy-start(bf16[392,1024]{1,0:T(8,128)(2,1)S(1)} %dynamic-slice_dynamic-update-slice_fusion) | copy-start | bytes 2408452
  92.9 585.8 %reduce-scatter.6.cloned.1.call-start = ((), (), s32[]{:S(2)}) async-start(), calls=%async_computation.6 | async-start | bytes 1310720 | tf_op jit(solution)/shard_map/reduce_scatter | solution.py:488
  93.6 4.8 collective-permute-start
  158.4 20.9 %collective-permute-start.1 = (bf16[8,128,256]{2,1,0:T(8,128)(2,1)S(1)}, bf16[8,128,256]{2,1,0:T(8,128)(2,1)S(1)}, u32[]{:S(2)}, u32[]{:S(2)}) collective-permute-start(bf16[8,128,256]{2,1,0:T(8,128)(2,1)S(1)} %slice.307), channel_id=1, source_target_pairs={{0,1},{4,5},{8,9},{12,13},{16,17},{20,21},{24,25},{28,29}} | collective-permute-start | bytes 1572872 | tf_op jit(solution)/shard_map/ppermute | solution.py:449
  181.4 0.7 collective-permute-start.2
  184.6 2.1 collective-permute-start.3
  307.6 31.3 %copy-start.9 = (f32[512,1024]{1,0:T(8,128)}, f32[512,1024]{1,0:T(8,128)S(1)}, u32[]{:S(2)}) copy-start(f32[512,1024]{1,0:T(8,128)S(1)} %get-tuple-element.170) | copy-start | bytes 6291460
  341.2 24.9 %copy-start.11 = (f32[512,1024]{1,0:T(8,128)}, f32[512,1024]{1,0:T(8,128)S(1)}, u32[]{:S(2)}) copy-start(f32[512,1024]{1,0:T(8,128)S(1)} %fusion.8) | copy-start | bytes 6291460
  372.6 15.9 %collective-permute-start.4 = (bf16[8,128,256]{2,1,0:T(8,128)(2,1)S(1)}, bf16[8,128,256]{2,1,0:T(8,128)(2,1)S(1)}, u32[]{:S(2)}, u32[]{:S(2)}) collective-permute-start(bf16[8,128,256]{2,1,0:T(8,128)(2,1)S(1)} %convert_element_type.218), channel_id=1, source_target_pairs={{3,2},{7,6},{11,10},{15,14},{19,18},{23,22},{27,26},{31,30}} | collective-permute-start | bytes 1572872 | tf_op jit(solution)/shard_map/ppermute | solution.py:449
  388.9 8.6 %collective-permute-start.5 = (bf16[8,128,256]{2,1,0:T(8,128)(2,1)S(1)}, bf16[8,128,256]{2,1,0:T(8,128)(2,1)S(1)}, u32[]{:S(2)}, u32[]{:S(2)}) collective-permute-start(bf16[8,128,256]{2,1,0:T(8,128)(2,1)S(1)} %fusion.16), channel_id=1, source_target_pairs={{2,1},{6,5},{10,9},{14,13},{18,17},{22,21},{26,25},{30,29}} | collective-permute-start | bytes 1572872 | tf_op jit(solution)/shard_map/ppermute | solution.py:449
  392.1 107.1 %collective-permute-start.18 = (bf16[4,2,2,128,1024]{4,3,2,1,0:T(8,128)(2,1)}, bf16[4,2,2,128,1024]{4,3,2,1,0:T(8,128)(2,1)}, u32[]{:S(2)}, u32[]{:S(2)}) collective-permute-start(bf16[4,2,2,128,1024]{4,3,2,1,0:T(8,128)(2,1)} %pad_maximum_fusion.2), channel_id=1, source_target_pairs={{0,4},{4,0},{8,12},{12,8},{16,20},{20,16},{24,28},{28,24},{1,5},{5... | collective-permute-start | bytes 12582920 | tf_op jit(solution)/shard_map/ppermute | solution.py:481
  397.8 37.1 %collective-permute-start.6 = (bf16[8,128,256]{2,1,0:T(8,128)(2,1)S(1)}, bf16[8,128,256]{2,1,0:T(8,128)(2,1)S(1)}, u32[]{:S(2)}, u32[]{:S(2)}) collective-permute-start(bf16[8,128,256]{2,1,0:T(8,128)(2,1)S(1)} %fusion.14), channel_id=1, source_target_pairs={{1,0},{5,4},{9,8},{13,12},{17,16},{21,20},{25,24},{29,28}} | collective-permute-start | bytes 1572872 | tf_op jit(solution)/shard_map/ppermute | solution.py:449
  403.4 170.4 %collective-permute-start.23 = (bf16[4,2,2,264,1024]{4,3,2,1,0:T(8,128)(2,1)}, bf16[4,2,2,264,1024]{4,3,2,1,0:T(8,128)(2,1)}, u32[]{:S(2)}, u32[]{:S(2)}) collective-permute-start(bf16[4,2,2,264,1024]{4,3,2,1,0:T(8,128)(2,1)} %pad_maximum_fusion), channel_id=1, source_target_pairs={{0,4},{4,0},{8,12},{12,8},{16,20},{20,16},{24,28},{28,24},{1,5},{5... | collective-permute-start | bytes 25952264 | tf_op jit(solution)/shard_map/ppermute | solution.py:481
  499.2 36.9 %collective-permute-start.13 = (bf16[4,2,2,32,4096]{4,3,1,0,2:T(8,128)(2,1)}, bf16[4,2,2,32,4096]{4,3,1,0,2:T(8,128)(2,1)}, u32[]{:S(2)}, u32[]{:S(2)}) collective-permute-start(bf16[4,2,2,32,4096]{4,3,1,0,2:T(8,128)(2,1)} %bitcast.229), channel_id=1, source_target_pairs={{0,4},{4,0},{8,12},{12,8},{16,20},{20,16},{24,28},{28,24},{1,5},{5... | collective-permute-start | bytes 12582920 | tf_op jit(solution)/shard_map/ppermute | solution.py:481
  507.6 25.7 %collective-permute-start.21 = (bf16[4,2,128,512]{3,2,1,0:T(8,128)(2,1)}, bf16[4,2,128,512]{3,2,1,0:T(8,128)(2,1)}, u32[]{:S(2)}, u32[]{:S(2)}) collective-permute-start(bf16[4,2,128,512]{3,2,1,0:T(8,128)(2,1)} %dynamic-slice_bitcast_fusion.12), channel_id=1, source_target_pairs={{0,16},{4,20},{8,24},{12,28},{16,0},{20,4},{24,8},{28,12},{1,17},{... | collective-permute-start | bytes 3145736 | tf_op jit(solution)/shard_map/ppermute | solution.py:468
  509.3 26.8 %copy-start.4 = (bf16[4,2,2,1,32,4096]{5,4,3,2,1,0:T(8,128)(2,1)S(1)}, bf16[4,2,2,1,32,4096]{5,4,3,2,1,0:T(8,128)(2,1)}, u32[]{:S(2)}) copy-start(bf16[4,2,2,1,32,4096]{5,4,3,2,1,0:T(8,128)(2,1)} %get-tuple-element.126) | copy-start | bytes 12582916
  509.4 31.9 %collective-permute-start.19 = (bf16[4,2,128,512]{3,2,1,0:T(8,128)(2,1)S(1)}, bf16[4,2,128,512]{3,2,1,0:T(8,128)(2,1)S(1)}, u32[]{:S(2)}, u32[]{:S(2)}) collective-permute-start(bf16[4,2,128,512]{3,2,1,0:T(8,128)(2,1)S(1)} %dynamic-slice_bitcast_fusion.13), channel_id=1, source_target_pairs={{0,8},{4,12},{8,0},{12,4},{16,24},{20,28},{24,16},{28,20},{1,9},{5... | collective-permute-start | bytes 3145736 | tf_op jit(solution)/shard_map/ppermute | solution.py:468
  534.7 14.9 %collective-permute-start.22 = (bf16[4,128,512]{2,1,0:T(8,128)(2,1)S(1)}, bf16[4,128,512]{2,1,0:T(8,128)(2,1)S(1)}, u32[]{:S(2)}, u32[]{:S(2)}) collective-permute-start(bf16[4,128,512]{2,1,0:T(8,128)(2,1)S(1)} %dynamic-slice_bitcast_fusion.19), channel_id=1, source_target_pairs={{0,8},{4,12},{8,0},{12,4},{16,24},{20,28},{24,16},{28,20},{1,9},{5... | collective-permute-start | bytes 1572872 | tf_op jit(solution)/shard_map/ppermute | solution.py:468
  540.5 30.1 %collective-permute-start.14 = (bf16[4,2,32,2048]{3,2,1,0:T(8,128)(2,1)}, bf16[4,2,32,2048]{3,2,1,0:T(8,128)(2,1)}, u32[]{:S(2)}, u32[]{:S(2)}) collective-permute-start(bf16[4,2,32,2048]{3,2,1,0:T(8,128)(2,1)} %dynamic-slice_bitcast_fusion.18), channel_id=1, source_target_pairs={{0,8},{4,12},{8,0},{12,4},{16,24},{20,28},{24,16},{28,20},{1,9},{5... | collective-permute-start | bytes 3145736 | tf_op jit(solution)/shard_map/ppermute | solution.py:468
  541.4 14.9 %collective-permute-start.20 = (bf16[4,128,512]{2,1,0:T(8,128)(2,1)S(1)}, bf16[4,128,512]{2,1,0:T(8,128)(2,1)S(1)}, u32[]{:S(2)}, u32[]{:S(2)}) collective-permute-start(bf16[4,128,512]{2,1,0:T(8,128)(2,1)S(1)} %dynamic-slice_bitcast_fusion.20), channel_id=1, source_target_pairs={{0,16},{4,20},{8,24},{12,28},{16,0},{20,4},{24,8},{28,12},{1,17},{... | collective-permute-start | bytes 1572872 | tf_op jit(solution)/shard_map/ppermute | solution.py:468
  545.3 39.0 %collective-permute-start.16 = (bf16[4,2,32,2048]{3,2,1,0:T(8,128)(2,1)}, bf16[4,2,32,2048]{3,2,1,0:T(8,128)(2,1)}, u32[]{:S(2)}, u32[]{:S(2)}) collective-permute-start(bf16[4,2,32,2048]{3,2,1,0:T(8,128)(2,1)} %bitcast.230), channel_id=1, source_target_pairs={{0,16},{4,20},{8,24},{12,28},{16,0},{20,4},{24,8},{28,12},{1,17},{... | collective-permute-start | bytes 3145736 | tf_op jit(solution)/shard_map/ppermute | solution.py:468
  557.5 121.9 %reduce-scatter.4.cloned.1.call-start = ((), (), s32[]{:S(2)}) async-start(), calls=%async_computation.5 | async-start | bytes 1310720 | tf_op jit(solution)/shard_map/reduce_scatter | solution.py:488
  572.1 18.1 %collective-permute-start.15 = (bf16[4,32,2048]{2,1,0:T(8,128)(2,1)S(1)}, bf16[4,32,2048]{2,1,0:T(8,128)(2,1)S(1)}, u32[]{:S(2)}, u32[]{:S(2)}) collective-permute-start(bf16[4,32,2048]{2,1,0:T(8,128)(2,1)S(1)} %dynamic-slice_bitcast_fusion.22), channel_id=1, source_target_pairs={{0,16},{4,20},{8,24},{12,28},{16,0},{20,4},{24,8},{28,12},{1,17},{... | collective-permute-start | bytes 1572872 | tf_op jit(solution)/shard_map/ppermute | solution.py:468
  583.9 64.0 %collective-permute-start.26 = (bf16[4,2,264,512]{3,2,1,0:T(8,128)(2,1)}, bf16[4,2,264,512]{3,2,1,0:T(8,128)(2,1)S(1)}, u32[]{:S(2)}, u32[]{:S(2)}) collective-permute-start(bf16[4,2,264,512]{3,2,1,0:T(8,128)(2,1)} %dynamic-slice_bitcast_fusion.6), channel_id=1, source_target_pairs={{0,16},{4,20},{8,24},{12,28},{16,0},{20,4},{24,8},{28,12},{1,17},{... | collective-permute-start | bytes 6488072 | tf_op jit(solution)/shard_map/ppermute | solution.py:468
  588.0 63.3 %collective-permute-start.24 = (bf16[4,2,264,512]{3,2,1,0:T(8,128)(2,1)}, bf16[4,2,264,512]{3,2,1,0:T(8,128)(2,1)}, u32[]{:S(2)}, u32[]{:S(2)}) collective-permute-start(bf16[4,2,264,512]{3,2,1,0:T(8,128)(2,1)} %dynamic-slice_bitcast_fusion.7), channel_id=1, source_target_pairs={{0,8},{4,12},{8,0},{12,4},{16,24},{20,28},{24,16},{28,20},{1,9},{5... | collective-permute-start | bytes 6488072 | tf_op jit(solution)/shard_map/ppermute | solution.py:468
  589.5 57.2 %collective-permute-start.17 = (bf16[4,32,2048]{2,1,0:T(8,128)(2,1)S(1)}, bf16[4,32,2048]{2,1,0:T(8,128)(2,1)S(1)}, u32[]{:S(2)}, u32[]{:S(2)}) collective-permute-start(bf16[4,32,2048]{2,1,0:T(8,128)(2,1)S(1)} %dynamic-slice_bitcast_fusion.21), channel_id=1, source_target_pairs={{0,8},{4,12},{8,0},{12,4},{16,24},{20,28},{24,16},{28,20},{1,9},{5... | collective-permute-start | bytes 1572872 | tf_op jit(solution)/shard_map/ppermute | solution.py:468
  647.8 72.2 %reduce-scatter.8.cloned.1.call-start = ((), (), s32[]{:S(2)}) async-start(), calls=%async_computation.7 | async-start | bytes 2703360 | tf_op jit(solution)/shard_map/reduce_scatter | solution.py:488
  649.8 23.2 %collective-permute-start.27 = (bf16[4,264,512]{2,1,0:T(8,128)(2,1)S(1)}, bf16[4,264,512]{2,1,0:T(8,128)(2,1)S(1)}, u32[]{:S(2)}, u32[]{:S(2)}) collective-permute-start(bf16[4,264,512]{2,1,0:T(8,128)(2,1)S(1)} %dynamic-slice_bitcast_fusion.10), channel_id=1, source_target_pairs={{0,8},{4,12},{8,0},{12,4},{16,24},{20,28},{24,16},{28,20},{1,9},{5... | collective-permute-start | bytes 3244040 | tf_op jit(solution)/shard_map/ppermute | solution.py:468
  654.0 22.9 %collective-permute-start.25 = (bf16[4,264,512]{2,1,0:T(8,128)(2,1)S(1)}, bf16[4,264,512]{2,1,0:T(8,128)(2,1)S(1)}, u32[]{:S(2)}, u32[]{:S(2)}) collective-permute-start(bf16[4,264,512]{2,1,0:T(8,128)(2,1)S(1)} %dynamic-slice_bitcast_fusion.11), channel_id=1, source_target_pairs={{0,16},{4,20},{8,24},{12,28},{16,0},{20,4},{24,8},{28,12},{1,17},{... | collective-permute-start | bytes 3244040 | tf_op jit(solution)/shard_map/ppermute | solution.py:468
  678.6 104.2 %all-gather.16.cloned.1.call-start = ((), (), s32[]{:S(2)}) async-start(), calls=%async_computation.9 | async-start | bytes 2359296 | tf_op jit(solution)/shard_map/all_gather | solution.py:489
  679.4 108.6 %all-gather.14.cloned.1.call-start = ((), (), s32[]{:S(2)}) async-start(), calls=%async_computation.8 | async-start | bytes 2359296 | tf_op jit(solution)/shard_map/all_gather | solution.py:489
  680.1 137.5 %all-gather.18.cloned.1.call-start = ((), (), s32[]{:S(2)}) async-start(), calls=%async_computation.10 | async-start | bytes 4866048 | tf_op jit(solution)/shard_map/all_gather | solution.py:489
  687.8 32.2 %copy-start.38 = (bf16[1024,8]{0,1:T(8,128)(2,1)S(1)}, bf16[1024,8]{0,1:T(8,128)(2,1)}, u32[]{:S(2)}) copy-start(bf16[1024,8]{0,1:T(8,128)(2,1)} %copy-done.37) | copy-start | bytes 49156
  687.8 32.3 %copy-start.40 = (bf16[1024,8]{0,1:T(8,128)(2,1)S(1)}, bf16[1024,8]{0,1:T(8,128)(2,1)}, u32[]{:S(2)}) copy-start(bf16[1024,8]{0,1:T(8,128)(2,1)} %copy-done.39) | copy-start | bytes 49156
  692.8 32.0 %copy-start.45 = (f32[4,2048]{1,0:T(4,128)S(1)}, f32[4,2048]{1,0:T(4,128)}, u32[]{:S(2)}) copy-start(f32[4,2048]{1,0:T(4,128)} %get-tuple-element.73) | copy-start | bytes 98308
  692.8 32.0 %copy-start.53 = (f32[4,1024]{1,0:T(4,128)S(1)}, f32[4,1024]{1,0:T(4,128)}, u32[]{:S(2)}) copy-start(f32[4,1024]{1,0:T(4,128)} %get-tuple-element.71) | copy-start | bytes 49156
  692.8 32.0 %copy-start.54 = (f32[4,1024]{1,0:T(4,128)S(1)}, f32[4,1024]{1,0:T(4,128)}, u32[]{:S(2)}) copy-start(f32[4,1024]{1,0:T(4,128)} %get-tuple-element.72) | copy-start | bytes 49156
  723.3 6.6 collective-permute-start.7
  745.3 1.4 collective-permute-start.8
  747.4 6.1 collective-permute-start.9
  754.5 9.7 %collective-permute-start.10 = (f32[280,128]{1,0:T(8,128)S(1)}, f32[280,128]{1,0:T(8,128)S(1)}, u32[]{:S(2)}, u32[]{:S(2)}) collective-permute-start(f32[280,128]{1,0:T(8,128)S(1)} %fusion.120), channel_id=1, source_target_pairs={{0,16},{4,20},{8,24},{12,28},{16,0},{20,4},{24,8},{28,12},{1,17},{... | collective-permute-start | bytes 430088 | tf_op jit(solution)/shard_map/ppermute | solution.py:502
  764.3 5.7 collective-permute-start.11
  770.0 7.9 collective-permute-start.12
  (65 other events, 390.6 us)
Sparse Core Ops, SparseCore 0:
  12.3 80.4 all-gather.9
  96.7 159.7 all-gather.11
Sparse Core Ops, SparseCore 1:
  18.7 38.7 all-reduce.4
  557.6 25.4 reduce-scatter.5
  647.9 25.0 reduce-scatter.3
  678.7 41.3 reduce-scatter.7
  722.0 27.0 all-gather.15
  750.9 27.7 all-gather.13
  780.4 37.1 all-gather.17

commit v2 on v1

--- a/solution.py
+++ b/solution.py
@@ -322,7 +322,7 @@
     def stack_shape(self, *shape, dtype=f32):
         return jax.ShapeDtypeStruct((self.heads,) + shape, dtype)
 
-    def call(self, kernel, in_specs, out_specs, out_shape, name, scratch=()):
+    def call(self, kernel, in_specs, out_specs, out_shape, name, micros, scratch=()):
         return pl.pallas_call(
             kernel,
             grid=(self.heads,),
@@ -331,6 +331,9 @@
             out_shape=out_shape,
             scratch_shapes=list(scratch),
             compiler_params=self.params,
+            cost_estimate=pl.CostEstimate(
+                flops=0, transcendentals=0, bytes_accessed=micros * self.count * self.heads * 768
+            ),
             name=name,
         )
 
@@ -351,6 +354,7 @@
                 self.stack_shape(DK, DK + DV),
             ],
             "delta_front",
+            41,
         )(ext, ext, ext, taps, taps, taps, col, row)
 
     def outputs(self, query, maps, start, wkey, wval, scores, col, gate_pre, gain):
@@ -367,6 +371,7 @@
                 self.wide_shape(DV, bf16),
             ],
             "delta_outputs",
+            18,
         )(query, maps, start, wkey, wval, scores, col, gate_pre, gain)
 
     def tail_back(self, dgated, mixed, gate_pre, gain, query, scores, wkey, steps, col):
@@ -386,6 +391,7 @@
                 self.stack_shape(DK, DV), self.stack_shape(1, DV),
             ],
             "delta_tail_back",
+            17,
         )(dgated, mixed, gate_pre, gain, query, scores, wkey, steps, col)
 
     def back(self, ext, taps, col, row, end, steps, into, inverse, wkey, wval, scores, states, fresh, dmixed, query, key):
@@ -412,6 +418,7 @@
                 jax.ShapeDtypeStruct((heads, count, 2), f32), jax.ShapeDtypeStruct((heads, 1, count), f32),
             ],
             "delta_back",
+            48,
             [
                 pltpu.VMEM((count, DK), f32), pltpu.VMEM((count, DK), f32), pltpu.VMEM((count, DV), f32),
                 pltpu.VMEM((PAD + count + 8, DV), f32),
@@ -428,6 +435,16 @@
 
 def gather_everywhere(block):
     return lax.all_gather(block, ("fsdp", "rep"), axis=0, tiled=True)
+
+
+def unpacked(parts, gather):
+    block = gather(jnp.concatenate(parts, 0))
+    block = block.reshape((-1,) + block.shape[-2:])
+    whole, at = [], 0
+    for part in parts:
+        whole.append(block[:, at : at + part.shape[0]].reshape(-1, part.shape[1]))
+        at += part.shape[0]
+    return whole
 
 
 def passed_along(block, distance):
@@ -468,29 +485,41 @@
     return kept + lax.ppermute(sent, "rep", partners(bit))
 
 
-def sum_to_owners(grads):
-    owners, reps = lax.axis_size("fsdp"), lax.axis_size("rep")
-    levels = reps.bit_length() - 1
-    width = grads[0].shape[1]
-    sizes = [grad.shape[0] // (owners * reps) for grad in grads]
-    pairs = [
-        halves(grad.reshape((owners,) + (2,) * levels + (size, width)), levels, 1)
-        for grad, size in zip(grads, sizes)
-    ]
-    kept, sent = [jnp.concatenate(side, -2) for side in zip(*pairs)]
-    block = kept + lax.ppermute(sent, "rep", partners(1))
-    left = block[..., : width // 2]
-    right = block[..., width // 2 :]
-    for level in range(1, levels):
-        left = halve(left, levels - level, 1 << level)
-        right = halve(right, 1, 1 << (levels - level))
-    block = jnp.concatenate([left, right], -1).reshape(-1, width)
-    block = lax.psum_scatter(block, "fsdp", scatter_dimension=0, tiled=True)
-    block = lax.all_gather(block, "rep", axis=0)
+class OwnerSums:
+    def __init__(self, grads):
+        self.owners, self.reps = lax.axis_size("fsdp"), lax.axis_size("rep")
+        self.levels = self.reps.bit_length() - 1
+        self.width = grads[0].shape[1]
+        self.sizes = [grad.shape[0] // (self.owners * self.reps) for grad in grads]
+        cut = (self.owners,) + (2,) * self.levels
+        pairs = [
+            halves(grad.reshape(cut + (size, self.width)), self.levels, 1)
+            for grad, size in zip(grads, self.sizes)
+        ]
+        kept, sent = [jnp.concatenate(side, -2) for side in zip(*pairs)]
+        self.block = kept + lax.ppermute(sent, "rep", partners(1))
+
+    def halve_level(self, level):
+        if level == 1:
+            self.left = self.block[..., : self.width // 2]
+            self.right = self.block[..., self.width // 2 :]
+        self.left = halve(self.left, self.levels - level, 1 << level)
+        self.right = halve(self.right, 1, 1 << (self.levels - level))
+
+    def scatter(self, *earlier):
+        block = jnp.concatenate([self.left, self.right], -1).reshape(-1, self.width)
+        for other in earlier:
+            block, other.block = lax.optimization_barrier((block, other.block))
+        self.block = lax.psum_scatter(block, "fsdp", scatter_dimension=0, tiled=True)
+
+
+def shared(groups):
+    block = lax.all_gather(jnp.concatenate([group.block for group in groups], 0), "rep", axis=0)
     sums, at = [], 0
-    for size in sizes:
-        sums.append(block[:, at : at + size].reshape(-1, width).astype(f32))
-        at += size
+    for group in groups:
+        for size in group.sizes:
+            sums.append(block[:, at : at + size].reshape(-1, group.width).astype(f32))
+            at += size
     return sums
 
 
@@ -552,21 +581,19 @@
         jnp.concatenate([rep_piece(w, share) for w in (w_query, w_key, w_value)], 1)
     )
     gate_pieces = rep_piece(w_gate, share)
-    parts = [
-        gate_pieces[:, :width],
-        gate_pieces[:, width:],
-        rep_piece(w_out, w_out.shape[0] // reps),
-        rep_piece(w_ffgate.T, w_ffgate.shape[1] // reps),
-        rep_piece(w_ffup.T, w_ffup.shape[1] // reps),
-        rep_piece(w_ffdown, w_ffdown.shape[0] // reps),
-    ]
-    packed, w_qkv = lax.optimization_barrier((jnp.concatenate(parts, 0), w_qkv))
-    rest = gather_everywhere(packed).reshape(owners * reps, -1, width)
-    whole, at = [], 0
-    for part in parts:
-        whole.append(rest[:, at : at + part.shape[0]].reshape(-1, width))
-        at += part.shape[0]
-    gate_left, gate_right, out_full, ffgate_t, ffup_t, ffdown_full = whole
+    gate_left, gate_right, out_full, ffgate_t, ffup_t, ffdown_full = unpacked(
+        [
+            gate_pieces[:, :width],
+            gate_pieces[:, width:],
+            rep_piece(w_out, w_out.shape[0] // reps),
+            rep_piece(w_ffgate.T, w_ffgate.shape[1] // reps),
+            rep_piece(w_ffup.T, w_ffup.shape[1] // reps),
+            rep_piece(w_ffdown, w_ffdown.shape[0] // reps),
+        ],
+        lambda block: lax.all_gather(
+            lax.optimization_barrier((block, w_qkv))[0], ("fsdp", "rep")
+        ),
+    )
 
     small = [norm_mix, norm_ffn, norm_head, w_beta.reshape(-1), w_decay.reshape(-1), conv_weight.reshape(-1)]
     small_full = lax.all_gather(jnp.concatenate(small), "fsdp", axis=0)
@@ -586,6 +613,7 @@
     normed_f32, mix_pull = jax.vjp(rms_scale, inputs, mix_gain)
     normed = normed_f32.astype(bf16)
     normed_ext = jnp.concatenate([rms_scale(ahead, mix_gain).astype(bf16), normed], 0)
+    normed_ext, taps, w_qkv = lax.optimization_barrier((normed_ext, taps, w_qkv))
     projected = matmul_low(normed_ext, w_qkv)
     gates_pre = matmul_low(normed, w_beta_decay)
     beta_pre, decay_pre = gates_pre[:, :head_count], gates_pre[:, head_count:]
@@ -627,23 +655,32 @@
     )
     end_grad = carried_states(transit, own_grad, True)
 
-    ffdown_grad, ffgate_grad, ffup_grad = sum_to_owners([
+    ffn_sums = OwnerSums([
         matmul_tn(swiglu_out, out_low).astype(bf16),
         matmul_tn(gate_low, normed_ffn).astype(bf16),
         matmul_tn(up_low, normed_ffn).astype(bf16),
     ])
-    out_weight_grad, gate_left_grad, gate_right_grad = sum_to_owners([
+    ffn_sums.halve_level(1)
+    mixer_sums = OwnerSums([
         matmul_tn(gated_out, residual_low).astype(bf16),
         matmul_tn(normed, dgate_low[:, :width]).astype(bf16),
         matmul_tn(normed, dgate_low[:, width:]).astype(bf16),
     ])
+    end_grad, ffn_sums.left, ffn_sums.right, mixer_sums.block = lax.optimization_barrier(
+        (end_grad, ffn_sums.left, ffn_sums.right, mixer_sums.block)
+    )
+    for level in range(2, ffn_sums.levels):
+        ffn_sums.halve_level(level)
+    mixer_sums.halve_level(1)
 
     dxq, dxk, dxv, dtap_q, dtap_k, dtap_v, dcol, drow = calls.back(
         projected, taps, col, row, end_grad, steps, into, inverse, wkey, wval, scores, states, fresh,
         dmixed, query, key,
     )
     dprojected = jnp.concatenate([dxq, dxk, dxv], 1)
-    (qkv_grad,) = sum_to_owners([matmul_tn(normed_ext, dprojected).astype(bf16)])
+    column_blocks = [dprojected[:, at : at + width] for at in range(0, dprojected.shape[1], width)]
+    qkv_sums = OwnerSums([matmul_tn(normed_ext, block).astype(bf16) for block in column_blocks])
+    qkv_sums.halve_level(1)
     coming = passed_along(dprojected[PAD - KW + 1 : PAD], -1)
     own_low = dprojected[PAD:]
     edge_rows = lax.dynamic_slice_in_dim(own_low, edge_place, KW - 1, 0).astype(f32) + coming.astype(f32)
@@ -658,13 +695,27 @@
         + matmul_nt(dgate_low[:, width:], gate_right)
         + matmul_high(gates_grad, w_beta_decay.astype(f32).T)
     )
-    input_part, mix_gain_grad = mix_pull(normed_grad)
-    grad_tokens = residual_grad + input_part
-
     gates_weight_grad = lax.dot_general(
         normed.astype(f32), gates_grad, (((0,), (0,)), ((), ())), precision=highest,
         preferred_element_type=f32,
     )
+    qkv_sums.left, qkv_sums.right, normed_grad, gates_weight_grad = lax.optimization_barrier(
+        (qkv_sums.left, qkv_sums.right, normed_grad, gates_weight_grad)
+    )
+    ffn_sums.scatter()
+    for level in range(2, mixer_sums.levels):
+        mixer_sums.halve_level(level)
+    mixer_sums.scatter(ffn_sums)
+    for level in range(2, qkv_sums.levels):
+        qkv_sums.halve_level(level)
+    qkv_sums.scatter(mixer_sums)
+    (
+        ffdown_grad, ffgate_grad, ffup_grad, out_weight_grad, gate_left_grad, gate_right_grad, *qkv_grads
+    ) = shared([ffn_sums, mixer_sums, qkv_sums])
+    qkv_grad = jnp.concatenate(qkv_grads, 1)
+    input_part, mix_gain_grad = mix_pull(normed_grad)
+    grad_tokens = residual_grad + input_part
+
     dtaps = jnp.concatenate([dtap_q, dtap_k, dtap_v], 1)
     small = [
         mix_gain_grad, ffn_gain_grad, jnp.sum(dgain, 0).reshape(-1), gates_weight_grad.reshape(-1),

time: 845 us -> 810 us (0.959)
  waiting for transfers between devices: 374 us -> 316 us
  other arithmetic: 63 us -> 80.1 us
    ppermute x12, waiting for transfers between devices: 124 us -> 35.4 us  [halve(): return kept + lax.ppermute(sent, 'rep', partners(bit))]
    all_gather x2 -> x1, waiting for transfers between devices: 136 us -> 69.3 us  [gather_everywhere(): return lax.all_gather(block, ('fsdp', 'rep'), axis=0, tiled=True)]
    all_gather x3 -> x2, waiting for transfers between devices: 25 us -> 81 us  [the longest x1 65.5 us: on_device(): lax.all_gather(lax.optimization_barrier((block, w_qkv))[0], ('fsdp', 'rep'))]
    reduce_scatter x3, waiting for transfers between devices: 26 us -> 59.1 us  [scatter(): lax.psum_scatter(block, 'fsdp', scatter_dimension=0, tiled=True)]
    concatenate x5 -> x9, other arithmetic: 10.4 us -> 17.9 us  [the longest x3 10.4 us: __init__(): kept, sent = [jnp.concatenate(side, -2) for side in zip(*pairs)]]
    dot_general x7 -> x10, matrix products: 24 us -> 31.5 us  [matmul_tn(): lax.dot_general(left, right, (((0,), (0,)), ((), ())), preferred_element_...]
    squeeze x6 -> x10, local copies, waits for them, and re-layouts: 11.8 us -> 17.9 us  [halves(): lax.dynamic_index_in_dim(block, mine, axis, keepdims=False)]
    unnamed x171 -> x199, local copies, waits for them, and re-layouts: 21.5 us -> 26.6 us
  transfers between devices with their start and end apart: 37 -> 35, of which waited for: 18 -> 17; matrix products, arithmetic and copies ran while one was open for 22% -> 22% of each run, Pallas kernels for 11% -> 7%
where the time goes in v2:
time: 810 us; the launch traced here: 800 us
  waiting for transfers between devices  316 us (39%)
  Pallas kernels  124 us (15%)
  matrix products  120 us (15%)
  local copies, waits for them, and re-layouts  110 us (14%)
  other arithmetic  80.1 us (10%)
  starting transfers between devices  30.2 us (4%)
  between operations  19 us (2%)
    all_gather x1, waiting for transfers between devices, gather_everywhere(): return lax.all_gather(block, ('fsdp', 'rep'), axis=0, tiled=True)  69.3 us
    all_gather x1, waiting for transfers between devices, on_device(): lax.all_gather(lax.optimization_barrier((block, w_qkv))[0], ('fsdp', 'rep'))  65.5 us
    reduce_scatter x3, waiting for transfers between devices, scatter(): lax.psum_scatter(block, 'fsdp', scatter_dimension=0, tiled=True)  59.1 us
    ppermute x6, waiting for transfers between devices, carried_states(): arrived = lax.ppermute(moved.astype(bf16), 'fsdp', [(source, target)])  51.6 us
    pallas_call x1, Pallas kernels, back(): self.call(back_kernel, self.ext_specs + self.tap_specs + [self.col, self....  48.1 us
    dot_general x7, matrix products, matmul_nt(): lax.dot_general(left, right, (((1,), (1,)), ((), ())), preferred_element_...  42.4 us
    pallas_call x1, Pallas kernels, front(): self.call(front_kernel, self.ext_specs + self.tap_specs + [self.col, self...  40.8 us
    ppermute x12, waiting for transfers between devices, halve(): return kept + lax.ppermute(sent, 'rep', partners(bit))  35.4 us
  transfers between devices with their start and end apart: 35, of which 17 were waited for; matrix products, arithmetic and copies ran while one was open for 22% of the time, Pallas kernels for 7%

profile of v2, /device:TPU:0, one launch (start us, length us, event | category | flops | bytes accessed | tf_op | source)
XLA Modules:
  0.0 799.7 jit_solution(12224674709065384947)
XLA Ops:
  24.2 69.3 %all-gather.7.cloned.1.call-done = bf16[1024,4096]{1,0:T(8,128)(2,1)} async-done(((bf16[32,4096]{1,0:T(8,128)(2,1)}), bf16[1024,4096]{1,0:T(8,128)(2,1)}) %all-gather.7.cloned.1.call-update) | async-done | bytes 8388624 | tf_op jit(solution)/shard_map/all_gather | solution.py:437
  94.3 3.4 collective-permute-start
  107.7 10.2 %fusion.77.xq.xk.xv = f32[528,4096]{1,0:T(8,128)} fusion(bf16[528,1024]{1,0:T(8,128)(2,1)S(1)} %pad_maximum_fusion.5, bf16[1024,4096]{1,0:T(8,128)(2,1)} %all-gather.7.cloned.1.call-done), kind=kOutput, calls=%fused_computation.227 | convolution fusion | flops 4429185024 | bytes 18120704 | tf_op jit(solution)/shard_map/dot_general | solution.py:537
  117.9 40.8 %delta_front.1 = (f32[512,1024]{1,0:T(8,128)}, f32[512,1024]{1,0:T(8,128)}, f32[8,4,128,128]{3,2,1,0:T(8,128)}, f32[512,1024]{1,0:T(8,128)}, f32[512,2048]{1,0:T...) custom-call(f32[528,4096]{1,0:T(8,128)} %fusion.77.xq.xk.xv, ...), custom_call_target="tpu_custom_call" | custom-call | bytes 128974848 | tf_op jit(solution)/shard_map/delta_front/pallas_call | solution.py:342
  160.0 4.2 collective-permute-start.1
  164.3 17.0 %collective-permute-done.1 = bf16[8,128,256]{2,1,0:T(8,128)(2,1)S(1)} collective-permute-done((bf16[8,128,256]{2,1,0:T(8,128)(2,1)S(1)}, bf16[8,128,256]{2,1,0:T(8,128)(2,1)S(1)}, u32[]{:S(2)}, u32[]{:S(2)}) %collective-permute-start.1) | collective-permute-done | bytes 524320 | tf_op jit(solution)/shard_map/ppermute | solution.py:466
  190.5 65.5 %all-gather.9.cloned.1.call-done = bf16[12544,1024]{1,0:T(8,128)(2,1)} async-done(((bf16[392,1024]{1,0:T(8,128)(2,1)}), bf16[12544,1024]{1,0:T(8,128)(2,1)}) %all-gather.9.cloned.1.call-update) | async-done | bytes 25690128 | tf_op jit(solution)/shard_map/all_gather | solution.py:593
  256.0 4.9 slice.229
  261.0 2.7 fusion.67
  263.7 14.6 %fusion.66 = (bf16[32,88,1024]{2,1,0:T(8,128)(2,1)}, bf16[32,88,1024]{2,1,0:T(8,128)(2,1)}, bf16[32,88,1024]{2,1,0:T(8,128)(2,1)}) fusion(bf16[32,392,1024]{2,1,0:T(8,128)(2,1)} %bitcast.264), kind=kLoop, calls=%fused_computation.216 | loop fusion | bytes 34603008 | tf_op jit(solution)/shard_map/slice | solution.py:445
  280.9 2.7 pad_maximum_fusion.1.gate_ref
  283.5 18.3 %delta_outputs.1 = (f32[512,2048]{1,0:T(8,128)}, f32[8,4,128,256]{3,2,1,0:T(8,128)}, f32[512,2048]{1,0:T(8,128)}, bf16[512,2048]{1,0:T(8,128)(2,1)}) custom-call(f32[512,1024]{1,0:T(8,128)} %get-tuple-element.63.q_ref, f32[8,4,128,384]{3,2,1,0:T(8,128)} %get-tuple-element.64.map_ref, f32[8,128,256]{2,1,0:T(8,128)} %convert_add_fusion.3.start_ref, ...), custom_call_target="tpu_custom_call" | custom-call | bytes 56623104 | tf_op jit(solution)/shard_map/delta_outputs/pallas_call | solution.py:362
  301.9 5.4 multiply_reduce_fusion.2
  307.6 5.0 fusion.81
  312.6 5.0 fusion.80
  317.6 10.4 %multiply_convert_fusion = (bf16[512,2816]{1,0:T(8,128)(2,1)}, bf16[512,2816]{1,0:T(8,128)(2,1)}, bf16[512,2816]{1,0:T(8,128)(2,1)}) fusion(f32[512,2816]{1,0:T(8,128)} %fusion.80, f32[512,2816]{1,0:T(8,128)} %fusion.81, bf16[2816,1024]{1,0:T(8,128)(2,1)S(1)} %bitcast.281, bf16[512,1024]{1,0:T(8,128)(2,1)S(1)} %copy-done.42, f32[512]{0:T(512)S(1)} %fusion.55), kind=kOutput, calls=%fused_computation.6 | convolution fusion | flops 2977431552 | bytes 27002880 | tf_op jit(solution)/shard_map/dot_general | solution.py:545
  328.0 5.7 convolution_convert_fusion.2
  333.7 3.5 convolution_convert_fusion
  342.2 3.4 convolution_convert_fusion.1
  348.2 4.0 pad_maximum_fusion
  352.4 5.5 fusion.82
  357.9 3.5 multiply_reduce_fusion
  363.6 4.4 fusion.26.dgated_ref
  368.0 16.5 %delta_tail_back.1 = (bf16[512,2048]{1,0:T(8,128)(2,1)}, f32[512,2048]{1,0:T(8,128)}, f32[8,4,128,256]{3,2,1,0:T(8,128)}, f32[8,128,256]{2,1,0:T(8,128)}, f32[8,1,256]{2,1,0:T(1,128)}) custom-call(f32[512,2048]{1,0:T(8,128)} %fusion.26.dgated_ref, f32[512,2048]{1,0:T(8,128)} %get-tuple-element.71.mixed_ref, f32[512,2048]{1,0:T(8,128)} %pad_maximum_fusion.1.gate_ref, ...), custom_call_target="tpu_custom_call" | custom-call | bytes 53477376 | tf_op jit(solution)/shard_map/delta_tail_back/pallas_call | solution.py:379
  403.4 8.0 %maximum_add_fusion = bf16[4,2,2,264,1024]{4,3,2,1,0:T(8,128)(2,1)S(1)} fusion(bf16[4,2,2,264,1024]{4,3,2,1,0:T(8,128)(2,1)} %collective-permute-done.7, bf16[4,2,2,88,1024]{4,3,2,1,0:T(8,128)(2,1)} %get-tuple-element.167, bf16[4,2,2,88,1024]{4,3,2,1,0:T(8,128)(2,1)} %get-tuple-element.165, bf16[4,2,2,88,1024]{4,3,2,1,0:T(8,128)(2,1)} %get-tuple-element.163), kind=kLoop, calls=%fused_computation | loop fusion | flops 34603008 | bytes 25952256 | tf_op jit(solution)/shard_map/add | solution.py:500
  411.4 2.6 fusion.68
  425.8 2.6 fusion.19
  428.5 34.5 %collective-permute-done.6 = bf16[8,128,256]{2,1,0:T(8,128)(2,1)S(1)} collective-permute-done((bf16[8,128,256]{2,1,0:T(8,128)(2,1)S(1)}, bf16[8,128,256]{2,1,0:T(8,128)(2,1)S(1)}, u32[]{:S(2)}, u32[]{:S(2)}) %collective-permute-start.6) | collective-permute-done | bytes 524320 | tf_op jit(solution)/shard_map/ppermute | solution.py:466
  464.2 5.8 maximum_add_fusion.1
  473.6 48.1 %delta_back.1 = (bf16[528,1024]{1,0:T(8,128)(2,1)}, bf16[528,1024]{1,0:T(8,128)(2,1)}, bf16[528,2048]{1,0:T(8,128)(2,1)}, f32[4,1024]{1,0:T(4,128)}, f32[4,1024]...) custom-call(f32[528,4096]{1,0:T(8,128)} %fusion.77.xq.xk.xv, ...), custom_call_target="tpu_custom_call" | custom-call | bytes 150994944 | tf_op jit(solution)/shard_map/delta_back/pallas_call | solution.py:401
  521.7 4.5 convolution_convert_fusion.4
  526.3 3.2 convolution_convert_fusion.5
  529.4 3.2 convolution_convert_fusion.7
  556.4 5.3 reduce_window_sum.23
  564.1 4.0 pad_maximum_fusion.3
  581.1 14.5 %collective-permute-done.22 = bf16[4,2,128,512]{3,2,1,0:T(8,128)(2,1)} collective-permute-done((bf16[4,2,128,512]{3,2,1,0:T(8,128)(2,1)}, bf16[4,2,128,512]{3,2,1,0:T(8,128)(2,1)}, u32[]{:S(2)}, u32[]{:S(2)}) %collective-permute-start.22) | collective-permute-done | bytes 1048608 | tf_op jit(solution)/shard_map/ppermute | solution.py:485
  603.5 7.0 collective-permute-done.23
  614.1 3.7 maximum_add_fusion.2
  622.8 27.9 %reduce-scatter.4.cloned.1.call-done = bf16[264,1024]{1,0:T(8,128)(2,1)} async-done(((bf16[1056,1024]{1,0:T(8,128)(2,1)}), bf16[264,1024]{1,0:T(8,128)(2,1)}) %reduce-scatter.4.cloned.1.call-update) | async-done | bytes 540688 | tf_op jit(solution)/shard_map/reduce_scatter | solution.py:513
  650.8 12.4 %add_add_fusion.2 = f32[512,1024]{1,0:T(8,128)} fusion(f32[512,1024]{1,0:T(8,128)} %fusion.39, f32[512,1024]{1,0:T(8,128)} %fusion.19, f32[512,1024]{1,0:T(8,128)} %fusion.22, bf16[512,4096]{1,0:T(8,128)(2,1)} %dynamic_update_slice.3, bf16[1024,4096]{1,0:T(8,128)(2,1)} %all-gather.7.cloned.1.call-done), kind=kOutput, calls=%fused_computation.48 | convolution fusion | flops 4296540160 | bytes 20971520 | tf_op jit(solution)/shard_map/dot_general | solution.py:545
  669.0 10.2 %collective-permute-done.27 = bf16[4,128,512]{2,1,0:T(8,128)(2,1)S(1)} collective-permute-done((bf16[4,128,512]{2,1,0:T(8,128)(2,1)S(1)}, bf16[4,128,512]{2,1,0:T(8,128)(2,1)S(1)}, u32[]{:S(2)}, u32[]{:S(2)}) %collective-permute-start.27) | collective-permute-done | bytes 524320 | tf_op jit(solution)/shard_map/ppermute | solution.py:485
  682.2 31.2 %reduce-scatter.8.cloned.1.call-done = bf16[128,1024]{1,0:T(8,128)(2,1)} async-done(((bf16[512,1024]{1,0:T(8,128)(2,1)}), bf16[128,1024]{1,0:T(8,128)(2,1)}) %reduce-scatter.8.cloned.1.call-update) | async-done | bytes 262160 | tf_op jit(solution)/shard_map/reduce_scatter | solution.py:513
  722.2 7.3 collective-permute-done.16
  732.1 7.8 multiply_convert_fusion.2
  740.0 5.1 collective-permute-done.18
  747.0 5.1 collective-permute-done.19
  756.9 15.4 %all-gather.11.cloned.1.call-done = bf16[4160,1024]{1,0:T(8,128)(2,1)} async-done(((bf16[520,1024]{1,0:T(8,128)(2,1)}), bf16[4160,1024]{1,0:T(8,128)(2,1)}) %all-gather.11.cloned.1.call-update) | async-done | bytes 8519696 | tf_op jit(solution)/shard_map/all_gather | solution.py:517
  775.8 2.7 fusion.69
  (412 shorter events, 182.3 us)
Async XLA Ops:
  8.0 86.2 %copy-start.3 = (bf16[512,1024]{1,0:T(8,128)(2,1)S(1)}, bf16[512,1024]{1,0:T(8,128)(2,1)}, u32[]{:S(2)}) copy-start(bf16[512,1024]{1,0:T(8,128)(2,1)} %param.19) | copy-start | bytes 3145732
  8.1 85.5 %all-gather.7.cloned.1.call-start = ((), (), s32[]{:S(2)}) async-start(), calls=%async_computation.3 | async-start | bytes 8650752 | tf_op jit(solution)/shard_map/all_gather | solution.py:437
  10.9 87.2 %copy-start.72 = (f32[8]{0:T(128)S(1)}, f32[8]{0:T(128)}, u32[]{:S(2)}) copy-start(f32[8]{0:T(128)} %param.29) | copy-start | bytes 100
  10.9 88.3 %all-reduce.5.cloned.1.call-start = ((), (), s32[]{:S(2)}) async-start(), calls=%async_computation.9 | async-start | bytes 143360
  18.6 237.4 %all-gather.9.cloned.1.call-start = ((), (), s32[]{:S(2)}) async-start(), calls=%async_computation.7 | async-start | bytes 26492928 | tf_op jit(solution)/shard_map/all_gather | solution.py:593
  24.2 69.3 %copy-start.43 = (bf16[392,1024]{1,0:T(8,128)(2,1)}, bf16[392,1024]{1,0:T(8,128)(2,1)S(1)}, u32[]{:S(2)}) copy-start(bf16[392,1024]{1,0:T(8,128)(2,1)S(1)} %dynamic-slice_dynamic-update-slice_fusion) | copy-start | bytes 2408452
  93.5 557.1 %reduce-scatter.4.cloned.1.call-start = ((), (), s32[]{:S(2)}) async-start(), calls=%async_computation.4 | async-start | bytes 2703360 | tf_op jit(solution)/shard_map/reduce_scatter | solution.py:513
  94.3 4.8 collective-permute-start
  160.0 21.3 %collective-permute-start.1 = (bf16[8,128,256]{2,1,0:T(8,128)(2,1)S(1)}, bf16[8,128,256]{2,1,0:T(8,128)(2,1)S(1)}, u32[]{:S(2)}, u32[]{:S(2)}) collective-permute-start(bf16[8,128,256]{2,1,0:T(8,128)(2,1)S(1)} %slice.322), channel_id=1, source_target_pairs={{0,1},{4,5},{8,9},{12,13},{16,17},{20,21},{24,25},{28,29}} | collective-permute-start | bytes 1572872 | tf_op jit(solution)/shard_map/ppermute | solution.py:466
  183.0 0.7 collective-permute-start.2
  186.2 2.1 collective-permute-start.3
  307.3 54.1 %copy-start.9 = (f32[512,1024]{1,0:T(8,128)}, f32[512,1024]{1,0:T(8,128)S(1)}, u32[]{:S(2)}) copy-start(f32[512,1024]{1,0:T(8,128)S(1)} %get-tuple-element.204) | copy-start | bytes 6291460
  352.2 51.2 %collective-permute-start.7 = (bf16[4,2,2,264,1024]{4,3,2,1,0:T(8,128)(2,1)}, bf16[4,2,2,264,1024]{4,3,2,1,0:T(8,128)(2,1)}, u32[]{:S(2)}, u32[]{:S(2)}) collective-permute-start(bf16[4,2,2,264,1024]{4,3,2,1,0:T(8,128)(2,1)} %pad_maximum_fusion), channel_id=1, source_target_pairs={{0,4},{4,0},{8,12},{12,8},{16,20},{20,16},{24,28},{28,24},{1,5},{5... | collective-permute-start | bytes 25952264 | tf_op jit(solution)/shard_map/ppermute | solution.py:500
  399.0 65.2 %collective-permute-start.10 = (bf16[4,2,2,128,1024]{4,3,2,1,0:T(8,128)(2,1)}, bf16[4,2,2,128,1024]{4,3,2,1,0:T(8,128)(2,1)}, u32[]{:S(2)}, u32[]{:S(2)}) collective-permute-start(bf16[4,2,2,128,1024]{4,3,2,1,0:T(8,128)(2,1)} %pad_maximum_fusion.2), channel_id=1, source_target_pairs={{0,4},{4,0},{8,12},{12,8},{16,20},{20,16},{24,28},{28,24},{1,5},{5... | collective-permute-start | bytes 12582920 | tf_op jit(solution)/shard_map/ppermute | solution.py:500
  399.4 1.1 collective-permute-start.4
  402.7 17.5 %collective-permute-start.5 = (bf16[8,128,256]{2,1,0:T(8,128)(2,1)}, bf16[8,128,256]{2,1,0:T(8,128)(2,1)S(1)}, u32[]{:S(2)}, u32[]{:S(2)}) collective-permute-start(bf16[8,128,256]{2,1,0:T(8,128)(2,1)} %fusion.16), channel_id=1, source_target_pairs={{2,1},{6,5},{10,9},{14,13},{18,17},{22,21},{26,25},{30,29}} | collective-permute-start | bytes 1572872 | tf_op jit(solution)/shard_map/ppermute | solution.py:466
  416.9 53.2 %collective-permute-start.8 = (bf16[4,2,264,512]{3,2,1,0:T(8,128)(2,1)}, bf16[4,2,264,512]{3,2,1,0:T(8,128)(2,1)}, u32[]{:S(2)}, u32[]{:S(2)}) collective-permute-start(bf16[4,2,264,512]{3,2,1,0:T(8,128)(2,1)} %dynamic-slice_bitcast_fusion.7), channel_id=1, source_target_pairs={{0,8},{4,12},{8,0},{12,4},{16,24},{20,28},{24,16},{28,20},{1,9},{5... | collective-permute-start | bytes 6488072 | tf_op jit(solution)/shard_map/ppermute | solution.py:485
  420.0 51.9 %collective-permute-start.9 = (bf16[4,2,264,512]{3,2,1,0:T(8,128)(2,1)S(1)}, bf16[4,2,264,512]{3,2,1,0:T(8,128)(2,1)S(1)}, u32[]{:S(2)}, u32[]{:S(2)}) collective-permute-start(bf16[4,2,264,512]{3,2,1,0:T(8,128)(2,1)S(1)} %dynamic-slice_bitcast_fusion.6), channel_id=1, source_target_pairs={{0,16},{4,20},{8,24},{12,28},{16,0},{20,4},{24,8},{28,12},{1,17},{... | collective-permute-start | bytes 6488072 | tf_op jit(solution)/shard_map/ppermute | solution.py:485
  421.8 41.3 %collective-permute-start.6 = (bf16[8,128,256]{2,1,0:T(8,128)(2,1)S(1)}, bf16[8,128,256]{2,1,0:T(8,128)(2,1)S(1)}, u32[]{:S(2)}, u32[]{:S(2)}) collective-permute-start(bf16[8,128,256]{2,1,0:T(8,128)(2,1)S(1)} %fusion.14), channel_id=1, source_target_pairs={{1,0},{5,4},{9,8},{13,12},{17,16},{21,20},{25,24},{29,28}} | collective-permute-start | bytes 1572872 | tf_op jit(solution)/shard_map/ppermute | solution.py:466
  425.8 38.4 %copy-start.21 = (bf16[4,2,2,32,1024]{4,3,2,1,0:T(8,128)(2,1)S(1)}, bf16[4,2,2,32,1024]{4,3,2,1,0:T(8,128)(2,1)}, u32[]{:S(2)}) copy-start(bf16[4,2,2,32,1024]{4,3,2,1,0:T(8,128)(2,1)} %get-tuple-element.185) | copy-start | bytes 3145732
  425.8 38.4 %copy-start.22 = (bf16[4,2,2,32,1024]{4,3,2,1,0:T(8,128)(2,1)S(1)}, bf16[4,2,2,32,1024]{4,3,2,1,0:T(8,128)(2,1)}, u32[]{:S(2)}) copy-start(bf16[4,2,2,32,1024]{4,3,2,1,0:T(8,128)(2,1)} %get-tuple-element.183) | copy-start | bytes 3145732
  428.5 35.7 %copy-start.13 = (bf16[4,2,2,64,1024]{4,3,2,1,0:T(8,128)(2,1)S(1)}, bf16[4,2,2,64,1024]{4,3,2,1,0:T(8,128)(2,1)}, u32[]{:S(2)}) copy-start(bf16[4,2,2,64,1024]{4,3,2,1,0:T(8,128)(2,1)} %get-tuple-element.173) | copy-start | bytes 6291460
  473.6 48.2 %copy-start.38 = (bf16[528,1024]{1,0:T(8,128)(2,1)S(1)}, bf16[528,1024]{1,0:T(8,128)(2,1)}, u32[]{:S(2)}) copy-start(bf16[528,1024]{1,0:T(8,128)(2,1)} %copy-done.37) | copy-start | bytes 3244036
  539.0 33.3 %collective-permute-start.25 = (bf16[4,264,512]{2,1,0:T(8,128)(2,1)}, bf16[4,264,512]{2,1,0:T(8,128)(2,1)}, u32[]{:S(2)}, u32[]{:S(2)}) collective-permute-start(bf16[4,264,512]{2,1,0:T(8,128)(2,1)} %dynamic-slice_bitcast_fusion.10), channel_id=1, source_target_pairs={{0,8},{4,12},{8,0},{12,4},{16,24},{20,28},{24,16},{28,20},{1,9},{5... | collective-permute-start | bytes 3244040 | tf_op jit(solution)/shard_map/ppermute | solution.py:485
  540.5 33.7 %collective-permute-start.24 = (bf16[4,264,512]{2,1,0:T(8,128)(2,1)}, bf16[4,264,512]{2,1,0:T(8,128)(2,1)}, u32[]{:S(2)}, u32[]{:S(2)}) collective-permute-start(bf16[4,264,512]{2,1,0:T(8,128)(2,1)} %dynamic-slice_bitcast_fusion.11), channel_id=1, source_target_pairs={{0,16},{4,20},{8,24},{12,28},{16,0},{20,4},{24,8},{28,12},{1,17},{... | collective-permute-start | bytes 3244040 | tf_op jit(solution)/shard_map/ppermute | solution.py:485
  562.8 38.2 %collective-permute-start.14 = (bf16[3,4096]{1,0:T(4,128)(2,1)}, bf16[3,4096]{1,0:T(4,128)(2,1)S(1)}, u32[]{:S(2)}, u32[]{:S(2)}) collective-permute-start(bf16[3,4096]{1,0:T(4,128)(2,1)} %slice.239), channel_id=1, source_target_pairs={{1,0},{2,1},{3,2},{5,4},{6,5},{7,6},{9,8},{10,9},{11,10},{13,12},{... | collective-permute-start | bytes 73736 | tf_op jit(solution)/shard_map/ppermute | solution.py:453
  568.1 46.0 %collective-permute-start.11 = (bf16[4,2,2,128,1024]{4,3,2,1,0:T(8,128)(2,1)}, bf16[4,2,2,128,1024]{4,3,2,1,0:T(8,128)(2,1)}, u32[]{:S(2)}, u32[]{:S(2)}) collective-permute-start(bf16[4,2,2,128,1024]{4,3,2,1,0:T(8,128)(2,1)} %pad_maximum_fusion.3), channel_id=1, source_target_pairs={{0,4},{4,0},{8,12},{12,8},{16,20},{20,16},{24,28},{28,24},{1,5},{5... | collective-permute-start | bytes 12582920 | tf_op jit(solution)/shard_map/ppermute | solution.py:500
  570.7 24.9 %collective-permute-start.22 = (bf16[4,2,128,512]{3,2,1,0:T(8,128)(2,1)}, bf16[4,2,128,512]{3,2,1,0:T(8,128)(2,1)}, u32[]{:S(2)}, u32[]{:S(2)}) collective-permute-start(bf16[4,2,128,512]{3,2,1,0:T(8,128)(2,1)} %dynamic-slice_bitcast_fusion.12), channel_id=1, source_target_pairs={{0,16},{4,20},{8,24},{12,28},{16,0},{20,4},{24,8},{28,12},{1,17},{... | collective-permute-start | bytes 3145736 | tf_op jit(solution)/shard_map/ppermute | solution.py:485
  572.2 26.1 %collective-permute-start.20 = (bf16[4,2,128,512]{3,2,1,0:T(8,128)(2,1)}, bf16[4,2,128,512]{3,2,1,0:T(8,128)(2,1)}, u32[]{:S(2)}, u32[]{:S(2)}) collective-permute-start(bf16[4,2,128,512]{3,2,1,0:T(8,128)(2,1)} %dynamic-slice_bitcast_fusion.13), channel_id=1, source_target_pairs={{0,8},{4,12},{8,0},{12,4},{16,24},{20,28},{24,16},{28,20},{1,9},{5... | collective-permute-start | bytes 3145736 | tf_op jit(solution)/shard_map/ppermute | solution.py:485
  577.3 104.5 %reduce-scatter.6.cloned.1.call-start = ((), (), s32[]{:S(2)}) async-start(), calls=%async_computation.5 | async-start | bytes 1310720 | tf_op jit(solution)/shard_map/reduce_scatter | solution.py:513
  597.8 12.7 %collective-permute-start.23 = (bf16[4,128,512]{2,1,0:T(8,128)(2,1)}, bf16[4,128,512]{2,1,0:T(8,128)(2,1)S(1)}, u32[]{:S(2)}, u32[]{:S(2)}) collective-permute-start(bf16[4,128,512]{2,1,0:T(8,128)(2,1)} %dynamic-slice_bitcast_fusion.30), channel_id=1, source_target_pairs={{0,8},{4,12},{8,0},{12,4},{16,24},{20,28},{24,16},{28,20},{1,9},{5... | collective-permute-start | bytes 1572872 | tf_op jit(solution)/shard_map/ppermute | solution.py:485
  600.5 12.4 %collective-permute-start.21 = (bf16[4,128,512]{2,1,0:T(8,128)(2,1)}, bf16[4,128,512]{2,1,0:T(8,128)(2,1)S(1)}, u32[]{:S(2)}, u32[]{:S(2)}) collective-permute-start(bf16[4,128,512]{2,1,0:T(8,128)(2,1)} %dynamic-slice_bitcast_fusion.31), channel_id=1, source_target_pairs={{0,16},{4,20},{8,24},{12,28},{16,0},{20,4},{24,8},{28,12},{1,17},{... | collective-permute-start | bytes 1572872 | tf_op jit(solution)/shard_map/ppermute | solution.py:485
  619.6 43.5 %collective-permute-start.12 = (bf16[4,2,128,512]{3,2,1,0:T(8,128)(2,1)S(1)}, bf16[4,2,128,512]{3,2,1,0:T(8,128)(2,1)}, u32[]{:S(2)}, u32[]{:S(2)}) collective-permute-start(bf16[4,2,128,512]{3,2,1,0:T(8,128)(2,1)S(1)} %dynamic-slice_bitcast_fusion.15), channel_id=1, source_target_pairs={{0,8},{4,12},{8,0},{12,4},{16,24},{20,28},{24,16},{28,20},{1,9},{5... | collective-permute-start | bytes 3145736 | tf_op jit(solution)/shard_map/ppermute | solution.py:485
  622.3 42.2 %collective-permute-start.13 = (bf16[4,2,128,512]{3,2,1,0:T(8,128)(2,1)}, bf16[4,2,128,512]{3,2,1,0:T(8,128)(2,1)}, u32[]{:S(2)}, u32[]{:S(2)}) collective-permute-start(bf16[4,2,128,512]{3,2,1,0:T(8,128)(2,1)} %dynamic-slice_bitcast_fusion.14), channel_id=1, source_target_pairs={{0,16},{4,20},{8,24},{12,28},{16,0},{20,4},{24,8},{28,12},{1,17},{... | collective-permute-start | bytes 3145736 | tf_op jit(solution)/shard_map/ppermute | solution.py:485
  650.7 62.7 %reduce-scatter.8.cloned.1.call-start = ((), (), s32[]{:S(2)}) async-start(), calls=%async_computation.6 | async-start | bytes 1310720 | tf_op jit(solution)/shard_map/reduce_scatter | solution.py:513
  665.9 13.3 %collective-permute-start.27 = (bf16[4,128,512]{2,1,0:T(8,128)(2,1)S(1)}, bf16[4,128,512]{2,1,0:T(8,128)(2,1)S(1)}, u32[]{:S(2)}, u32[]{:S(2)}) collective-permute-start(bf16[4,128,512]{2,1,0:T(8,128)(2,1)S(1)} %dynamic-slice_bitcast_fusion.28), channel_id=1, source_target_pairs={{0,8},{4,12},{8,0},{12,4},{16,24},{20,28},{24,16},{28,20},{1,9},{5... | collective-permute-start | bytes 1572872 | tf_op jit(solution)/shard_map/ppermute | solution.py:485
  667.5 13.1 %collective-permute-start.26 = (bf16[4,128,512]{2,1,0:T(8,128)(2,1)S(1)}, bf16[4,128,512]{2,1,0:T(8,128)(2,1)S(1)}, u32[]{:S(2)}, u32[]{:S(2)}) collective-permute-start(bf16[4,128,512]{2,1,0:T(8,128)(2,1)S(1)} %dynamic-slice_bitcast_fusion.29), channel_id=1, source_target_pairs={{0,16},{4,20},{8,24},{12,28},{16,0},{20,4},{24,8},{28,12},{1,17},{... | collective-permute-start | bytes 1572872 | tf_op jit(solution)/shard_map/ppermute | solution.py:485
  679.3 34.1 %copy-start.44 = (bf16[264,1024]{1,0:T(8,128)(2,1)S(1)}, bf16[264,1024]{1,0:T(8,128)(2,1)}, u32[]{:S(2)}) copy-start(bf16[264,1024]{1,0:T(8,128)(2,1)} %reduce-scatter.4.cloned.1.call-done) | copy-start | bytes 1622020
  681.8 33.8 %copy-start.73 = (f32[8]{0:T(128)S(1)}, f32[8]{0:T(128)}, u32[]{:S(2)}) copy-start(f32[8]{0:T(128)} %param.29) | copy-start | bytes 100
  681.8 34.2 %copy-start.4 = (bf16[512,1024]{1,0:T(8,128)(2,1)S(1)}, bf16[512,1024]{1,0:T(8,128)(2,1)}, u32[]{:S(2)}) copy-start(bf16[512,1024]{1,0:T(8,128)(2,1)} %param.19) | copy-start | bytes 3145732
  681.8 34.2 %copy-start.53 = (f32[1,2,4,128]{3,1,2,0:T(2,128)S(1)}, f32[1,2,4,128]{3,1,2,0:T(2,128)}, u32[]{:S(2)}) copy-start(f32[1,2,4,128]{3,1,2,0:T(2,128)} %copy-done.52) | copy-start | bytes 12292
  681.9 34.2 %copy-start.55 = (f32[512]{0:T(512)S(1)}, f32[512]{0:T(512)}, u32[]{:S(2)}) copy-start(f32[512]{0:T(512)} %copy-done.54) | copy-start | bytes 6148
  681.9 90.4 %all-gather.11.cloned.1.call-start = ((), (), s32[]{:S(2)}) async-start(), calls=%async_computation.8 | async-start | bytes 9584640 | tf_op jit(solution)/shard_map/all_gather | solution.py:517
  718.7 1.4 collective-permute-start.15
  720.8 8.8 %collective-permute-start.16 = (f32[280,128]{1,0:T(8,128)}, f32[280,128]{1,0:T(8,128)}, u32[]{:S(2)}, u32[]{:S(2)}) collective-permute-start(f32[280,128]{1,0:T(8,128)} %fusion.63), channel_id=1, source_target_pairs={{0,8},{4,12},{8,0},{12,4},{16,24},{20,28},{24,16},{28,20},{1,9},{5... | collective-permute-start | bytes 430088 | tf_op jit(solution)/shard_map/ppermute | solution.py:531
  730.5 9.3 %collective-permute-start.17 = (f32[280,128]{1,0:T(8,128)S(1)}, f32[280,128]{1,0:T(8,128)S(1)}, u32[]{:S(2)}, u32[]{:S(2)}) collective-permute-start(f32[280,128]{1,0:T(8,128)S(1)} %fusion.125), channel_id=1, source_target_pairs={{0,16},{4,20},{8,24},{12,28},{16,0},{20,4},{24,8},{28,12},{1,17},{... | collective-permute-start | bytes 430088 | tf_op jit(solution)/shard_map/ppermute | solution.py:531
  739.9 5.2 collective-permute-start.18
  745.1 7.0 collective-permute-start.19
  (77 other events, 522.8 us)
Sparse Core Ops, SparseCore 0:
  12.7 80.7 all-gather.6
  97.3 158.6 all-gather.8
Sparse Core Ops, SparseCore 1:
  18.7 38.7 all-reduce.4
  577.4 73.3 reduce-scatter.3
  653.4 26.4 reduce-scatter.5
  682.8 30.5 reduce-scatter.7
  715.9 56.4 all-gather.10
